TPU v7x, 512 devices: a whole 4x8x8 slice. The times are simulated.
512 devices in a mesh: dom: 64 (over x, z, core), col: 8 (over y).
Axes of the slice: x: 4, y: 8, z: 8, core: 2. Of those that a mesh axis runs over, the one named last changes fastest.
Arguments:
- feats: bfloat16 [128, 131072], P('col', 'dom'), may hold values from -6 to 6
- part_len: int32 [64], P('dom'), may hold values from 1 to 2048, 98304 in all
- loc_vals: bfloat16 [1536, 128, 128], P('dom'), may hold values from -0.375 to 0.375
- loc_coord: int32 [1536, 2], P('dom'), may hold values from 0 to 15
- send_block: int32 [64, 64], P('dom'), may hold values from 0 to 15
- send_live: int32 [64, 64], P('dom'), may hold values 0 or 1
- rem_vals: bfloat16 [4096, 128, 128], P('dom'), may hold values from -0.375 to 0.375
- rem_dst: int32 [64, 64], P('dom'), may hold values from 0 to 15
- weight: bfloat16 [2, 128, 256], replicated, may hold values from -0.375 to 0.375
- bias: float32 [256], replicated, may hold values from -3 to 3
- cot: bfloat16 [256, 131072], P(None, ('dom', 'col')), may hold values from -6 to 6
Outputs:
- hidden: bfloat16 [256, 131072], P(None, ('dom', 'col'))
- grad_feats: float32 [128, 131072], P('col', 'dom')
- grad_weight: float32 [2, 128, 256], P(None, 'col')
- grad_bias: float32 [256], replicated
Inputs may be any that keep to these rules, and one draw needn't show every extreme that they name: `part_len`: one partition holds exactly 2048 live nodes. `loc_coord`: blocks may repeat; repeated blocks add.
All inputs are finite; a program needn't handle non-finite values. No bound on the sum of `part_len` or of `send_live` on one device may be relied on, other than what follows from the above.
Results may differ from a plain program's by a relative error of at most 0.014.
Values may be sent and summed in bfloat16 or wider, within the bound.
No kernel may reach another device: no remote copies, remote signals or barrier semaphores. Data moves between devices by JAX's collectives and lax.ppermute only.
A program may use at most 64 MiB of HBM per device.

v0:
```python
import jax
import jax.numpy as jnp
from jax import lax
from jax.sharding import PartitionSpec as P


def to_blocks(matrix, nblocks, width):
    return matrix.reshape(matrix.shape[0], nblocks, width).transpose(1, 0, 2)


def from_blocks(blocks):
    return blocks.transpose(1, 0, 2).reshape(blocks.shape[1], blocks.shape[0] * blocks.shape[2])


def shards(
    feats,
    part_len,
    loc_vals,
    loc_coord,
    send_block,
    send_live,
    rem_vals,
    rem_dst,
    weight,
    bias,
    cot,
):
    f32 = jnp.float32
    width = loc_vals.shape[1]
    slots = feats.shape[1]
    cols_here = feats.shape[0]
    nblocks = slots // width
    n_dom = lax.axis_size("dom")
    n_col = lax.axis_size("col")
    col_idx = lax.axis_index("col")
    rows_out = slots // n_col
    live_len = part_len[0]
    mask = (jnp.arange(slots, dtype=jnp.int32) < live_len).astype(f32)
    out_mask = (col_idx * rows_out + jnp.arange(rows_out, dtype=jnp.int32) < live_len).astype(f32)
    xm = jnp.where(mask[None, :] > 0, feats, jnp.zeros_like(feats))
    xblocks = to_blocks(xm, nblocks, width)
    rowids = jnp.arange(nblocks, dtype=jnp.int32)
    live_row = send_live[0]
    src_sel = (loc_coord[:, 0][None, :] == rowids[:, None]).astype(f32)
    dst_sel = (loc_coord[:, 1][None, :] == rowids[:, None]).astype(f32)
    rem_sel = (rem_dst[0][None, :] == rowids[:, None]).astype(f32)
    send_sel = (send_block[0][None, :] == rowids[:, None]).astype(f32) * live_row[None, :].astype(
        f32
    )
    picked = xblocks[send_block[0]]
    picked = jnp.where(live_row[:, None, None] > 0, picked, jnp.zeros_like(picked))
    arrived = lax.all_to_all(picked, "dom", split_axis=0, concat_axis=0, tiled=True)
    lterm = jnp.einsum(
        "kfs,ksd->kfd", xblocks[loc_coord[:, 0]], loc_vals, preferred_element_type=f32
    )
    rterm = jnp.einsum("qfs,qsd->qfd", arrived, rem_vals, preferred_element_type=f32)
    aggblocks = jnp.einsum("rk,kfd->rfd", dst_sel, lterm) + jnp.einsum(
        "rq,qfd->rfd", rem_sel, rterm
    )
    agg = (from_blocks(aggblocks) * mask[None, :]).astype(jnp.bfloat16)
    stacked = jnp.stack([xm, agg])
    wfull = weight.reshape(2 * weight.shape[1], weight.shape[2])
    factor = 1.0 / float(slots * n_dom) ** 0.5
    regrouped = lax.all_to_all(stacked, "col", split_axis=2, concat_axis=1, tiled=True)
    xfull = regrouped.reshape(wfull.shape[0], rows_out)
    z = (
        lax.dot_general(wfull, xfull, (((0,), (0,)), ((), ())), preferred_element_type=f32)
        + bias[:, None]
    )
    hidden = (jax.nn.silu(z) * out_mask[None, :]).astype(jnp.bfloat16)
    sig = jax.nn.sigmoid(z)
    dsilu = sig * (1.0 + z * (1.0 - sig))
    dz = (cot.astype(f32) * dsilu * out_mask[None, :]).astype(jnp.bfloat16)
    dx_rows = jnp.dot(wfull, dz, preferred_element_type=f32).reshape(2, weight.shape[1], rows_out)
    outgoing = jnp.stack(
        [dx_rows[0].astype(jnp.bfloat16), (dx_rows[1] * out_mask[None, :]).astype(jnp.bfloat16)]
    )
    returned = lax.all_to_all(outgoing, "col", split_axis=1, concat_axis=2, tiled=True)
    dw_rows = lax.dot_general(xfull, dz, (((1,), (1,)), ((), ())), preferred_element_type=f32)
    db_rows = jnp.sum(dz.astype(f32), axis=1)
    dw_sum, db_sum = lax.psum((dw_rows, db_rows), ("dom", "col"))
    grad_weight = lax.dynamic_slice_in_dim(
        (dw_sum * factor).reshape(2, weight.shape[1], weight.shape[2]),
        col_idx * cols_here,
        cols_here,
        1,
    )
    grad_bias = db_sum * factor
    direct = returned[0]
    dagg = returned[1]
    gblocks = to_blocks(dagg, nblocks, width)
    lback = jnp.einsum(
        "kft,kst->kfs", gblocks[loc_coord[:, 1]], loc_vals, preferred_element_type=f32
    )
    rback = jnp.einsum("qft,qst->qfs", gblocks[rem_dst[0]], rem_vals, preferred_element_type=f32)
    returned_terms = lax.all_to_all(
        rback.astype(jnp.bfloat16), "dom", split_axis=0, concat_axis=0, tiled=True
    ).astype(rback.dtype)
    backblocks = jnp.einsum("rk,kfs->rfs", src_sel, lback) + jnp.einsum(
        "rq,qfs->rfs", send_sel, returned_terms
    )
    grad_feats = (direct.astype(f32) + from_blocks(backblocks)) * mask[None, :]
    return (hidden, grad_feats, grad_weight, grad_bias)


def solution(mesh):
    placed = (
        P("col", "dom"),
        P("dom"),
        P("dom", None, None),
        P("dom", None),
        P("dom", None),
        P("dom", None),
        P("dom", None, None),
        P("dom", None),
        P(),
        P(),
        P(None, ("dom", "col")),
    )
    return jax.shard_map(
        shards,
        mesh=mesh,
        in_specs=placed,
        out_specs=(P(None, ("dom", "col")), P("col", "dom"), P(None, "col", None), P()),
        check_vma=False,
    )
```

profile of v0, /device:TPU:1, one launch (start us, length us, event | category | flops | bytes accessed | tf_op | source)
XLA Modules:
  0.0 348.1 jit_solution(5431782255574424256)
XLA Ops:
  7.2 0.0 copy-start
  7.2 0.0 copy-start.4
  7.2 0.0 copy-start.1
  8.0 0.9 fusion.13
  8.9 0.7 fusion.30
  9.6 0.7 compare_bitcast_fusion
  10.3 0.6 gather_fusion.1
  10.9 0.8 broadcast_select_fusion
  11.7 14.8 %all-to-all-start = ((bf16[64,16,128]{2,1,0:T(8,128)(2,1)}), bf16[64,16,128]{2,1,0:T(8,128)(2,1)S(1)}, u32[]{:S(2)}, u32[]{:S(2)}) async-start(bf16[64,16,128]{2,1,0:T(8,128)(2,1)} %broadcast_select_fusion), calls=%async_computation | async-start | bytes 524288 | tf_op jit(solution)/shard_map/all_to_all | solution.py:52
  26.6 1.3 slice_bitcast_fusion
  27.9 0.6 gather_fusion
  28.4 0.0 copy-done.4
  28.5 0.0 copy-done.1
  28.5 0.3 fusion.35
  28.8 9.8 %all-to-all-done = bf16[64,16,128]{2,1,0:T(8,128)(2,1)S(1)} async-done(((bf16[64,16,128]{2,1,0:T(8,128)(2,1)}), bf16[64,16,128]{2,1,0:T(8,128)(2,1)S(1)}, u32[]{:S(2)}, u32[]{:S(2)}) %all-to-all-start) | async-done | bytes 262176 | tf_op jit(solution)/shard_map/all_to_all | solution.py:52
  38.6 0.0 copy-done
  38.6 0.6 fusion.36
  39.2 0.0 copy-start.7
  39.2 0.2 fusion.2
  39.4 0.2 fusion.1
  39.7 0.7 copy.55
  40.4 1.7 reshape.209
  42.1 6.8 %all-to-all-start.1 = ((bf16[8,2,4096]{2,1,0:T(2,128)(2,1)}), bf16[8,2,4096]{2,1,0:T(2,128)(2,1)S(1)}, u32[]{:S(2)}, u32[]{:S(2)}) async-start(bf16[8,2,4096]{2,1,0:T(2,128)(2,1)} %reshape.209), calls=%async_computation.1 | async-start | bytes 262144 | tf_op jit(solution)/shard_map/all_to_all | solution.py:64
  48.9 0.6 compare_convert_fusion
  49.5 1.0 copy.58
  50.5 0.0 copy-done.7
  50.5 0.5 convert_bitcast_fusion
  51.1 5.7 %all-to-all-done.1 = bf16[8,2,4096]{2,1,0:T(2,128)(2,1)S(1)} async-done(((bf16[8,2,4096]{2,1,0:T(2,128)(2,1)}), bf16[8,2,4096]{2,1,0:T(2,128)(2,1)S(1)}, u32[]{:S(2)}, u32[]{:S(2)}) %all-to-all-start.1) | async-done | bytes 131104 | tf_op jit(solution)/shard_map/all_to_all | solution.py:64
  56.7 0.7 reshape.210
  57.4 0.6 copy.68
  58.1 1.3 convert_reduce_fusion
  59.3 1.1 convolution_bitcast_fusion
  60.4 0.8 fusion.11
  61.3 0.8 copy.59
  62.1 3.4 all-to-all-start.2
  65.4 0.0 all-reduce.2.cloned.1.call-start
  65.5 0.9 fusion.38
  66.4 0.0 all-reduce.2.cloned.1.call-update
  66.4 0.8 copy.66
  67.2 98.9 %psum.15 = f32[256]{0:T(256)S(1)} all-reduce(f32[256]{0:T(256)S(1)} %get-tuple-element.24), channel_id=1, replica_groups=mesh['dom'=64,'col'=8] {'dom','col'}, use_global_device_ids=true, to_apply=%region_2.3 | all-reduce | flops 256 | bytes 2048 | tf_op jit(solution)/shard_map/psum | solution.py:81
  166.0 0.6 broadcast_multiply_fusion.1
  166.6 0.0 all-to-all-done.2
  166.7 0.6 gather_fusion.3
  167.4 0.0 copy-start.2
  167.4 0.0 copy-start.5
  167.4 0.0 copy-start.6
  167.4 1.9 convolution_convert_fusion
  169.3 0.0 copy-start.3
  169.3 6.7 %all-to-all-start.3 = ((bf16[64,16,128]{2,1,0:T(8,128)(2,1)}), bf16[64,16,128]{2,1,0:T(8,128)(2,1)S(1)}, u32[]{:S(2)}, u32[]{:S(2)}) async-start(bf16[64,16,128]{2,1,0:T(8,128)(2,1)} %convolution_convert_fusion), calls=%async_computation.3 | async-start | bytes 524288 | tf_op jit(solution)/shard_map/all_to_all | solution.py:96
  176.0 161.5 %all-reduce.2.cloned.1.call-done = f32[256,256]{1,0:T(8,128)} async-done(((f32[256,256]{1,0:T(8,128)}), f32[256,256]{1,0:T(8,128)}) %all-reduce.2.cloned.1.call-update) | async-done | bytes 262160 | tf_op jit(solution)/shard_map/psum | solution.py:81
  337.5 1.0 broadcast_multiply_fusion
  338.5 0.6 constant_dynamic-slice_fusion
  339.1 0.6 gather_fusion.2
  339.7 0.0 copy-done.2
  339.7 0.5 fusion.37
  340.2 0.0 all-to-all-done.3
  340.2 0.0 copy-done.5
  340.2 0.0 copy-done.6
  340.2 0.2 fusion.4
  340.4 0.0 copy-done.3
  340.4 0.2 convolution_add_fusion.1
  340.6 0.7 fusion.8
  (17 shorter events, 0.2 us)
Async XLA Ops:
  7.2 31.4 %copy-start = (bf16[64,128,128]{2,1,0:T(8,128)(2,1)S(1)}, bf16[64,128,128]{2,1,0:T(8,128)(2,1)}, u32[]{:S(2)}) copy-start(bf16[64,128,128]{2,1,0:T(8,128)(2,1)} %param.17) | copy-start | bytes 6291460
  7.2 21.3 %copy-start.4 = (s32[1,64]{1,0:T(1,128)S(1)}, s32[1,64]{1,0:T(1,128)}, u32[]{:S(2)}) copy-start(s32[1,64]{1,0:T(1,128)} %param.18) | copy-start | bytes 772
  7.2 21.3 %copy-start.1 = (bf16[24,128,128]{2,1,0:T(8,128)(2,1)S(1)}, bf16[24,128,128]{2,1,0:T(8,128)(2,1)}, u32[]{:S(2)}) copy-start(bf16[24,128,128]{2,1,0:T(8,128)(2,1)} %param.13) | copy-start | bytes 2359300
  11.7 26.8 %all-to-all-start = ((bf16[64,16,128]{2,1,0:T(8,128)(2,1)}), bf16[64,16,128]{2,1,0:T(8,128)(2,1)S(1)}, u32[]{:S(2)}, u32[]{:S(2)}) async-start(bf16[64,16,128]{2,1,0:T(8,128)(2,1)} %broadcast_select_fusion), calls=%async_computation | async-start | bytes 524288 | tf_op jit(solution)/shard_map/all_to_all | solution.py:52
  39.2 11.3 %copy-start.7 = (s32[1,64]{1,0:T(1,128)S(1)}, s32[1,64]{1,0:T(1,128)}, u32[]{:S(2)}) copy-start(s32[1,64]{1,0:T(1,128)} %param.16) | copy-start | bytes 772
  42.1 14.6 %all-to-all-start.1 = ((bf16[8,2,4096]{2,1,0:T(2,128)(2,1)}), bf16[8,2,4096]{2,1,0:T(2,128)(2,1)S(1)}, u32[]{:S(2)}, u32[]{:S(2)}) async-start(bf16[8,2,4096]{2,1,0:T(2,128)(2,1)} %reshape.209), calls=%async_computation.1 | async-start | bytes 262144 | tf_op jit(solution)/shard_map/all_to_all | solution.py:64
  62.1 104.5 %all-to-all-start.2 = ((bf16[2,128,256]{2,0,1:T(2,128)(2,1)}), bf16[2,128,256]{2,0,1:T(2,128)(2,1)S(1)}, u32[]{:S(2)}, u32[]{:S(2)}) async-start(bf16[2,128,256]{2,0,1:T(2,128)(2,1)} %copy.59), calls=%async_computation.2 | async-start | bytes 262144 | tf_op jit(solution)/shard_map/all_to_all | solution.py:78
  65.4 272.1 %all-reduce.2.cloned.1.call-start = ((), (), s32[]{:S(2)}) async-start(), calls=%async_computation.4 | async-start | bytes 524288 | tf_op jit(solution)/shard_map/psum | solution.py:81
  167.4 172.3 %copy-start.2 = (bf16[24,128,128]{2,1,0:T(8,128)(2,1)S(1)}, bf16[24,128,128]{2,1,0:T(8,128)(2,1)}, u32[]{:S(2)}) copy-start(bf16[24,128,128]{2,1,0:T(8,128)(2,1)} %param.13) | copy-start | bytes 2359300
  167.4 172.8 %copy-start.5 = (s32[1,64]{1,0:T(1,128)S(1)}, s32[1,64]{1,0:T(1,128)}, u32[]{:S(2)}) copy-start(s32[1,64]{1,0:T(1,128)} %param.15) | copy-start | bytes 772
  167.4 172.8 %copy-start.6 = (bf16[64]{0:T(256)(128)(2,1)S(1)}, bf16[64]{0:T(256)(128)(2,1)}, u32[]{:S(2)}) copy-start(bf16[64]{0:T(256)(128)(2,1)} %convert_bitcast_fusion) | copy-start | bytes 388
  169.3 171.1 %copy-start.3 = (s32[24]{0:T(128)S(1)}, s32[24]{0:T(128)}, u32[]{:S(2)}) copy-start(s32[24]{0:T(128)} %get-tuple-element.31) | copy-start | bytes 292
  169.3 170.9 %all-to-all-start.3 = ((bf16[64,16,128]{2,1,0:T(8,128)(2,1)}), bf16[64,16,128]{2,1,0:T(8,128)(2,1)S(1)}, u32[]{:S(2)}, u32[]{:S(2)}) async-start(bf16[64,16,128]{2,1,0:T(8,128)(2,1)} %convolution_convert_fusion), calls=%async_computation.3 | async-start | bytes 524288 | tf_op jit(solution)/shard_map/all_to_all | solution.py:96
Sparse Core Ops, SparseCore 0:
  71.3 266.1 all-reduce.1
where the time goes:
time: 349 us; the launch traced here: 348 us
  waiting for transfers between devices  177 us (51%)
  blocking collectives  98.9 us (28%)
  starting transfers between devices  31.7 us (9%)
  between operations  15.2 us (4%)
  local copies, waits for them, and re-layouts  9.57 us (3%)
  other arithmetic  8.55 us (2%)
  matrix products  7.26 us (2%)
    psum x1, waiting for transfers between devices, shards(): dw_sum, db_sum = lax.psum((dw_rows, db_rows), ('dom', 'col'))  162 us
    psum x1, blocking collectives, shards(): dw_sum, db_sum = lax.psum((dw_rows, db_rows), ('dom', 'col'))  98.9 us
    all_to_all x1, starting transfers between devices, shards(): lax.all_to_all(picked, 'dom', split_axis=0, concat_axis=0, tiled=True)  14.8 us
    all_to_all x1, waiting for transfers between devices, shards(): lax.all_to_all(picked, 'dom', split_axis=0, concat_axis=0, tiled=True)  9.79 us
  transfers between devices with their start and end apart: 5, of which 3 were waited for; matrix products, arithmetic and copies ran while one was open for 3% of the time, Pallas kernels for 0%

commit v1 on v0

v1 whole, which is shorter than its diff:
```python
import jax
import jax.numpy as jnp
from jax import lax
from jax.experimental import pallas as pl
from jax.experimental.pallas import tpu as pltpu
from jax.sharding import PartitionSpec as P

F32 = jnp.float32
BF16 = jnp.bfloat16
NX, NZ, NCORE = 4, 8, 2
NDOM = NX * NZ * NCORE
NCOL = 8
NB = 16
W = 128
ROWS = 16
H = 256
LOC = 24
CHUNK = 16

SMEM = pl.BlockSpec(memory_space=pltpu.SMEM)
VMEM = pl.BlockSpec(memory_space=pltpu.VMEM)
ANY = pl.BlockSpec(memory_space=pl.ANY)
NT = (((1,), (1,)), ((), ()))
NN = (((1,), (0,)), ((), ()))


def dot(a, b, dims=NN):
    return lax.dot_general(a, b, dims, preferred_element_type=F32)


def call(body, out_shape, in_specs, scratch=(), flops=0, nbytes=0, out_specs=None, name=None, aliases=None):
    many = isinstance(out_shape, (list, tuple))
    return pl.pallas_call(
        body,
        out_shape=out_shape,
        in_specs=in_specs,
        out_specs=out_specs or ([VMEM] * len(out_shape) if many else VMEM),
        scratch_shapes=list(scratch),
        compiler_params=pltpu.CompilerParams(vmem_limit_bytes=24 * 2**20),
        cost_estimate=pl.CostEstimate(flops=flops, bytes_accessed=nbytes, transcendentals=0),
        input_output_aliases=aliases or {},
        name=name,
    )


def masked_block(feats, live, b):
    node = lax.broadcasted_iota(jnp.int32, (ROWS, W), 1) + b * W
    return jnp.where(node < live, feats[:, b * W : (b + 1) * W].astype(F32), 0.0).astype(BF16)


def pick_kernel(live, send_block, send_live, feats, out, xs):
    for b in range(NB):
        xs[b] = masked_block(feats, live[0], b)
    xs[NB] = jnp.zeros((ROWS, W), BF16)
    for q in range(NDOM):
        out[q] = xs[jnp.where(send_live[0, q] > 0, send_block[0, q], NB)]


def start_chunks(hbm, buf, sems, total):
    copies = []
    for i in range(total // CHUNK):
        part = pl.ds(i * CHUNK, CHUNK)
        copy = pltpu.make_async_copy(hbm.at[part], buf.at[part], sems.at[i])
        copy.start()
        copies.append(copy)
    return copies


def local_fwd_kernel(live, coord, feats, vals, out, xs):
    for b in range(NB):
        xs[b] = masked_block(feats, live[0], b)
    out[...] = jnp.zeros_like(out)
    for k in range(LOC):
        out[coord[k, 1]] += dot(xs[coord[k, 0]], vals[k])


def agg_kernel(live, rem_dst, feats, arrived, local, rem, out, acc, buf, sems):
    copies = start_chunks(rem, buf, sems, NDOM)
    acc[...] = local[...]
    for c in range(NCOL):
        for j in range(2):
            out[c, 0:ROWS, j * W : (j + 1) * W] = masked_block(feats, live[0], 2 * c + j)
    for q in range(NDOM):
        if q % CHUNK == 0:
            copies[q // CHUNK].wait()
        acc[rem_dst[0, q]] += dot(arrived[q], buf[q])
    for c in range(NCOL):
        for j in range(2):
            b = 2 * c + j
            node = lax.broadcasted_iota(jnp.int32, (ROWS, W), 1) + b * W
            mask = (node < live[0]).astype(F32)
            out[c, ROWS : 2 * ROWS, j * W : (j + 1) * W] = (acc[b] * mask).astype(BF16)


def dense_kernel(live, first, got, wt, w, bias, cot, hidden, out):
    node = lax.broadcasted_iota(jnp.int32, (H, H), 1) + first[0]
    mask = (node < live[0]).astype(F32)
    x = got[...].reshape(NCOL * 2 * ROWS, H)
    z = dot(wt[...], x) + bias[...]
    sig = 1.0 / (1.0 + jnp.exp(-z))
    hidden[...] = (z * sig * mask).astype(BF16)
    dz = (cot[...].astype(F32) * (sig * (1.0 + z * (1.0 - sig))) * mask).astype(BF16)
    dx = dot(w[...], dz)
    dw = dot(x, dz, NT)
    db = dot(jnp.ones((ROWS, H), BF16), dz, NT)
    mask_rows = mask[0:ROWS]
    for c in range(NCOL):
        r = c * 2 * ROWS
        out[c, 0:ROWS] = dx[r : r + ROWS].astype(BF16)
        out[c, ROWS : 2 * ROWS] = (dx[r + ROWS : r + 2 * ROWS] * mask_rows).astype(BF16)
        out[c, 2 * ROWS : 4 * ROWS] = dw[r : r + 2 * ROWS].astype(BF16)
        out[c, 4 * ROWS : 5 * ROWS] = db.astype(BF16)


def dw_kernel(got, out):
    dw = jnp.zeros((2 * ROWS, H), F32)
    db = jnp.zeros((ROWS, H), F32)
    for c in range(NCOL):
        dw = dw + got[c, 2 * ROWS : 4 * ROWS].astype(F32)
        db = db + got[c, 4 * ROWS : 5 * ROWS].astype(F32)
    tail = jnp.concatenate([db[0:1, 0:W], db[0:1, W : 2 * W], jnp.zeros((6, W), F32)], axis=0)
    for r in range(4):
        for h in range(2):
            part = dw[8 * r : 8 * r + 8, h * W : (h + 1) * W]
            out[2 * r + h] = jnp.concatenate([part, tail], axis=0).astype(BF16)


def load_grad_blocks(got, gs):
    for c in range(NCOL):
        rows = got[c, ROWS : 2 * ROWS]
        gs[2 * c] = rows[:, 0:W]
        gs[2 * c + 1] = rows[:, W : 2 * W]


def back_kernel(rem_dst, got, rem, out, gs, buf, sems):
    copies = start_chunks(rem, buf, sems, NDOM)
    load_grad_blocks(got, gs)
    for q in range(NDOM):
        if q % CHUNK == 0:
            copies[q // CHUNK].wait()
        out[q, 0:ROWS] = dot(gs[rem_dst[0, q]], buf[q], NT).astype(BF16)


def attach_kernel(sent, got, out, buf, sem):
    total = jnp.zeros((ROWS, W), F32)
    for g in range(NX * NCORE):
        total = total + got[g].astype(F32)
    total = total.astype(BF16)
    for q in range(NDOM):
        buf[q] = total
    copy = pltpu.make_async_copy(buf, out.at[:, ROWS : 2 * ROWS, :], sem)
    copy.start()
    copy.wait()


def local_bwd_kernel(coord, got, vals, out, gs):
    load_grad_blocks(got, gs)
    for c in range(NCOL):
        rows = got[c, 0:ROWS].astype(F32)
        out[2 * c] = rows[:, 0:W]
        out[2 * c + 1] = rows[:, W : 2 * W]
    for k in range(LOC):
        out[coord[k, 0]] += dot(gs[coord[k, 1]], vals[k], NT)


def final_kernel(factor, live, send_block, send_live, local, got, grad, gw, gb, acc):
    acc[0:NB] = local[...]
    for q in range(NDOM):
        b = jnp.where(send_live[0, q] > 0, send_block[0, q], NB)
        acc[b] += got[q, 0:ROWS].astype(F32)
    for b in range(NB):
        node = lax.broadcasted_iota(jnp.int32, (ROWS, W), 1) + b * W
        mask = (node < live[0]).astype(F32)
        grad[:, b * W : (b + 1) * W] = acc[b] * mask
    for x in range(NX):
        for core in range(NCORE):
            total = jnp.zeros((ROWS, W), F32)
            for z in range(NZ):
                total = total + got[(x * NZ + z) * NCORE + core, ROWS : 2 * ROWS].astype(F32)
            total = total * factor
            r = 8 * (x % 2)
            gw[x // 2, r : r + 8, core * W : (core + 1) * W] = total[0:8]
            if x == 0 and core == 0:
                gb[...] = total[8:10]


def shards(
    feats,
    part_len,
    loc_vals,
    loc_coord,
    send_block,
    send_live,
    rem_vals,
    rem_dst,
    weight,
    bias,
    cot,
):
    sds = jax.ShapeDtypeStruct
    slots = feats.shape[1]
    first = (lax.axis_index("col") * (slots // NCOL)).astype(jnp.int32).reshape(1)
    groups = [[(x * NZ + z) * NCORE + core for x in range(NX) for core in range(NCORE)] for z in range(NZ)]
    wr = weight.reshape(2, NCOL, ROWS, H).transpose(1, 0, 2, 3).reshape(NCOL * 2 * ROWS, H)
    wt = wr.T
    factor = 1.0 / float(slots * NDOM) ** 0.5
    rem_scratch = [pltpu.VMEM((NDOM, W, W), BF16), pltpu.SemaphoreType.DMA((NDOM // CHUNK,))]
    rem_flops = 2 * NDOM * ROWS * W * W
    rem_bytes = NDOM * W * W * 2

    picked = call(
        pick_kernel,
        sds((NDOM, ROWS, W), BF16),
        [SMEM, SMEM, SMEM, VMEM],
        [pltpu.VMEM((NB + 1, ROWS, W), BF16)],
        nbytes=320 * 1024,
        name="pick",
    )(part_len, send_block, send_live, feats)
    arrived = lax.all_to_all(picked, "dom", split_axis=0, concat_axis=0, tiled=True)
    local = call(
        local_fwd_kernel,
        sds((NB, ROWS, W), F32),
        [SMEM, SMEM, VMEM, VMEM],
        [pltpu.VMEM((NB, ROWS, W), BF16)],
        flops=2 * LOC * ROWS * W * W,
        nbytes=LOC * W * W * 2,
        name="local_fwd",
    )(part_len, loc_coord, feats, loc_vals)
    stacked = call(
        agg_kernel,
        sds((NCOL, 2 * ROWS, 2 * W), BF16),
        [SMEM, SMEM, VMEM, VMEM, VMEM, ANY],
        [pltpu.VMEM((NB, ROWS, W), F32)] + rem_scratch,
        flops=rem_flops,
        nbytes=rem_bytes,
        name="agg",
    )(part_len, rem_dst, feats, arrived, local, rem_vals)
    regrouped = lax.all_to_all(stacked, "col", split_axis=0, concat_axis=0, tiled=True)
    hidden, outgoing = call(
        dense_kernel,
        [sds((H, 2 * W), BF16), sds((NCOL, 5 * ROWS, 2 * W), BF16)],
        [SMEM, SMEM] + [VMEM] * 5,
        flops=3 * 2 * H**3,
        nbytes=2**20,
        name="dense",
    )(part_len, first, regrouped, wt, wr, bias.reshape(H, 1), cot)
    returned = lax.all_to_all(outgoing, "col", split_axis=0, concat_axis=0, tiled=True)
    dw_send = call(dw_kernel, sds((NX * NCORE, ROWS, W), BF16), [VMEM], nbytes=400 * 1024, name="dw")(returned)
    dw_got = lax.all_to_all(
        dw_send, "dom", split_axis=0, concat_axis=0, tiled=True, axis_index_groups=groups
    )
    terms = call(
        back_kernel,
        sds((NDOM, 2 * ROWS, W), BF16),
        [SMEM, VMEM, ANY],
        [pltpu.VMEM((NB, ROWS, W), BF16)] + rem_scratch,
        flops=rem_flops,
        nbytes=rem_bytes,
        name="back",
    )(rem_dst, returned, rem_vals)
    terms = call(
        attach_kernel,
        sds((NDOM, 2 * ROWS, W), BF16),
        [ANY, VMEM],
        [pltpu.VMEM((NDOM, ROWS, W), BF16), pltpu.SemaphoreType.DMA],
        out_specs=ANY,
        nbytes=256 * 1024,
        aliases={0: 0},
        name="attach",
    )(terms, dw_got)
    got = lax.all_to_all(terms, "dom", split_axis=0, concat_axis=0, tiled=True)
    local_back = call(
        local_bwd_kernel,
        sds((NB, ROWS, W), F32),
        [SMEM, VMEM, VMEM],
        [pltpu.VMEM((NB, ROWS, W), BF16)],
        flops=2 * LOC * ROWS * W * W,
        nbytes=LOC * W * W * 2,
        name="local_bwd",
    )(loc_coord, returned, loc_vals)

    def final_body(*refs):
        final_kernel(factor, *refs)

    grad_feats, grad_weight, grad_bias = call(
        final_body,
        [sds((ROWS, slots), F32), sds((2, ROWS, H), F32), sds((2, W), F32)],
        [SMEM, SMEM, SMEM, VMEM, VMEM],
        [pltpu.VMEM((NB + 1, ROWS, W), F32)],
        nbytes=2**20,
        name="final",
    )(part_len, send_block, send_live, local_back, got)
    return (hidden, grad_feats, grad_weight, grad_bias.reshape(H))


def solution(mesh):
    placed = (
        P("col", "dom"),
        P("dom"),
        P("dom", None, None),
        P("dom", None),
        P("dom", None),
        P("dom", None),
        P("dom", None, None),
        P("dom", None),
        P(),
        P(),
        P(None, ("dom", "col")),
    )
    return jax.shard_map(
        shards,
        mesh=mesh,
        in_specs=placed,
        out_specs=(P(None, ("dom", "col")), P("col", "dom"), P(None, "col", None), P()),
        check_vma=False,
    )
```

time: 349 us -> 105 us (0.30)
  waiting for transfers between devices: 177 us -> 33.3 us
  blocking collectives: 98.9 us -> 12.2 us
  between operations: 15.2 us -> 1.42 us
  Pallas kernels: 0 us -> 13.2 us
  other arithmetic: 8.55 us -> 0 us
  matrix products: 7.26 us -> 0 us
  starting transfers between devices: 31.7 us -> 35.5 us
    psum x1 -> x0, waiting for transfers between devices: 162 us -> none  [shards(): dw_sum, db_sum = lax.psum((dw_rows, db_rows), ('dom', 'col'))]
    psum x1 -> x0, blocking collectives: 98.9 us -> none  [shards(): dw_sum, db_sum = lax.psum((dw_rows, db_rows), ('dom', 'col'))]
    all_to_all x3, waiting for transfers between devices: 5.66 us -> 25.1 us  [the longest x1 16.1 us: shards(): got = lax.all_to_all(terms, 'dom', split_axis=0, concat_axis=0, tiled=True)]
    pallas_call x0 -> x9, Pallas kernels: none -> 13.2 us  [the longest x1 3.09 us: shards(): call(back_kernel, sds((NDOM, 2 * ROWS, W), BF16), [SMEM, VMEM, ANY], [plt...]
    all_to_all x0 -> x1, blocking collectives: none -> 12.2 us  [shards(): lax.all_to_all(outgoing, 'col', split_axis=0, concat_axis=0, tiled=True)]
    dot_general x11 -> x0, matrix products: 7.26 us -> none  [the longest x1 1.9 us: shards(): jnp.einsum('qft,qst->qfs', gblocks[rem_dst[0]], rem_vals, preferred_eleme...]
    all_to_all x3, starting transfers between devices: 16.9 us -> 20.6 us  [the longest x1 8.55 us: shards(): lax.all_to_all(dw_send, 'dom', split_axis=0, concat_axis=0, tiled=True, a...]
    unnamed x21 -> x33, local copies, waits for them, and re-layouts: 4.23 us -> 8 us
  transfers between devices with their start and end apart: 5 -> 4, of which waited for: 3 -> 4; matrix products, arithmetic and copies ran while one was open for 3% -> 1% of each run, Pallas kernels for 0% -> 5%
where the time goes in v1:
time: 105 us; the launch traced here: 104 us
  starting transfers between devices  35.5 us (34%)
  waiting for transfers between devices  33.3 us (32%)
  Pallas kernels  13.2 us (13%)
  blocking collectives  12.2 us (12%)
  local copies, waits for them, and re-layouts  8.24 us (8%)
  between operations  1.42 us (1%)
    all_to_all x1, waiting for transfers between devices, shards(): got = lax.all_to_all(terms, 'dom', split_axis=0, concat_axis=0, tiled=True)  16.1 us
    all_to_all x1, starting transfers between devices, shards(): lax.all_to_all(picked, 'dom', split_axis=0, concat_axis=0, tiled=True)  14.8 us
    all_to_all x1, blocking collectives, shards(): lax.all_to_all(outgoing, 'col', split_axis=0, concat_axis=0, tiled=True)  12.2 us
    all_to_all x1, starting transfers between devices, shards(): lax.all_to_all(dw_send, 'dom', split_axis=0, concat_axis=0, tiled=True, a...  8.55 us
    all_to_all x1, waiting for transfers between devices, shards(): lax.all_to_all(picked, 'dom', split_axis=0, concat_axis=0, tiled=True)  8.2 us
    unnamed x33, local copies, waits for them, and re-layouts  8 us
    all_to_all x1, waiting for transfers between devices, shards(): lax.all_to_all(stacked, 'col', split_axis=0, concat_axis=0, tiled=True)  7.5 us
    all_to_all x1, starting transfers between devices, shards(): lax.all_to_all(stacked, 'col', split_axis=0, concat_axis=0, tiled=True)  6.83 us
  transfers between devices with their start and end apart: 4, of which 4 were waited for; matrix products, arithmetic and copies ran while one was open for 1% of the time, Pallas kernels for 5%

profile of v1, /device:TPU:1, one launch (start us, length us, event | category | flops | bytes accessed | tf_op | source)
XLA Modules:
  0.0 103.9 jit_solution(11502640711181131554)
XLA Ops:
  1.3 0.0 copy-start.4
  1.3 0.8 copy-done.4
  2.1 0.0 copy-start.10
  2.1 0.7 copy-done.10
  2.8 0.0 copy-start.12
  2.8 0.7 copy-done.12
  3.4 1.3 %pick.1 = bf16[64,16,128]{2,1,0:T(8,128)(2,1)} custom-call(s32[1]{0:T(128)S(6)} %copy.26.live.refs_0_, s32[1,64]{1,0:T(1,128)S(1)} %copy-done.10, s32[1,64]{1,0:T(1,128)S(1)} %copy-done.12, bf16[16,2048]{1,0:T(8,128)(2,1)S(1)} %copy-done.4), custom_call_target="tpu_custom_call" | custom-call | bytes 327680 | tf_op jit(solution)/shard_map/pick/pallas_call | solution.py:211
  4.8 14.8 %all-to-all-start = ((bf16[64,16,128]{2,1,0:T(8,128)(2,1)}), bf16[64,16,128]{2,1,0:T(8,128)(2,1)S(1)}, u32[]{:S(2)}, u32[]{:S(2)}) async-start(bf16[64,16,128]{2,1,0:T(8,128)(2,1)} %pick.1), calls=%async_computation | async-start | bytes 524288 | tf_op jit(solution)/shard_map/all_to_all | solution.py:219
  19.6 0.8 copy.20.coord
  20.4 0.0 copy-start.2
  20.4 1.1 %copy-done.2 = bf16[24,128,128]{2,1,0:T(8,128)(2,1)S(1)} copy-done((bf16[24,128,128]{2,1,0:T(8,128)(2,1)S(1)}, bf16[24,128,128]{2,1,0:T(8,128)(2,1)}, u32[]{:S(2)}) %copy-start.2) | copy-done | bytes 786456
  21.5 0.0 copy-start.5
  21.5 0.8 copy-done.5
  22.4 0.0 copy-start.14
  22.4 0.0 copy-start.15
  22.4 0.0 copy-start.7
  22.4 1.1 %local_fwd.1.local = f32[16,16,128]{2,1,0:T(8,128)S(1)} custom-call(s32[1]{0:T(128)S(6)} %copy.26.live.refs_0_, s32[24,2]{1,0:T(8,128)S(1)} %copy.20.coord, bf16[16,2048]{1,0:T(8,128)(2,1)S(1)} %copy-done.5, bf16[24,128,128]{2,1,0:T(8,128)(2,1)S(1)} %copy-done.2), custom_call_target="tpu_custom_call" | custom-call | flops 12582912 | bytes 786432 | tf_op jit(solution)/shard_map/local_fwd/pallas_call | solution.py:220
  23.4 8.2 %all-to-all-done.arrived = bf16[64,16,128]{2,1,0:T(8,128)(2,1)S(1)} async-done(((bf16[64,16,128]{2,1,0:T(8,128)(2,1)}), bf16[64,16,128]{2,1,0:T(8,128)(2,1)S(1)}, u32[]{:S(2)}, u32[]{:S(2)}) %all-to-all-start) | async-done | bytes 262176 | tf_op jit(solution)/shard_map/all_to_all | solution.py:219
  31.6 0.0 copy-start
  31.6 1.6 %copy-done = bf16[64,128,128]{2,1,0:T(8,128)(2,1)S(1)} copy-done((bf16[64,128,128]{2,1,0:T(8,128)(2,1)S(1)}, bf16[64,128,128]{2,1,0:T(8,128)(2,1)}, u32[]{:S(2)}) %copy-start) | copy-done | bytes 2097176
  33.2 0.0 copy-start.6
  33.2 0.8 copy-done.6
  34.1 0.0 copy-start.8
  34.1 0.7 copy-done.8
  34.7 0.0 copy-start.1
  34.7 0.0 copy-start.9
  34.7 2.4 %agg.1 = bf16[8,32,256]{2,1,0:T(8,128)(2,1)} custom-call(s32[1]{0:T(128)S(6)} %copy.26.live.refs_0_, s32[1,64]{1,0:T(1,128)S(1)} %copy-done.8, bf16[16,2048]{1,0:T(8,128)(2,1)S(1)} %copy-done.6, bf16[64,16,128]{2,1,0:T(8,128)(2,1)S(1)} %all-to-all-done.arrived, f32[16,16,128]{2,1,0:T(8,128)S(1)} %local_fwd.1.local, bf16[64,128,128]{2,1,0:T(8,128)(2,1)S(1)} %copy-done), custom_call_target="tpu_custom_call" | custom-call | flops 33554432 | bytes 2097152 | tf_op jit(solution)/shard_map/agg/pallas_call | solution.py:229
  37.2 6.8 %all-to-all-start.1 = ((bf16[8,32,256]{2,1,0:T(8,128)(2,1)}), bf16[8,32,256]{2,1,0:T(8,128)(2,1)S(1)}, u32[]{:S(2)}, u32[]{:S(2)}) async-start(bf16[8,32,256]{2,1,0:T(8,128)(2,1)} %agg.1), calls=%async_computation.1 | async-start | bytes 262144 | tf_op jit(solution)/shard_map/all_to_all | solution.py:238
  44.0 0.0 copy-done.14
  44.0 0.1 copy.22.wt
  44.1 0.0 copy-done.15
  44.1 0.1 copy.23.bias
  44.3 7.5 %all-to-all-done.1.got = bf16[8,32,256]{2,1,0:T(8,128)(2,1)S(1)} async-done(((bf16[8,32,256]{2,1,0:T(8,128)(2,1)}), bf16[8,32,256]{2,1,0:T(8,128)(2,1)S(1)}, u32[]{:S(2)}, u32[]{:S(2)}) %all-to-all-start.1) | async-done | bytes 131104 | tf_op jit(solution)/shard_map/all_to_all | solution.py:238
  51.8 0.0 copy-done.7
  51.8 1.0 dense.1
  52.8 12.2 %all_to_all.25.got = bf16[8,80,256]{2,1,0:T(8,128)(2,1)S(1)} all-to-all(bf16[8,80,256]{2,1,0:T(8,128)(2,1)S(1)} %get-tuple-element.10), channel_id=1, replica_groups=mesh['dom'=64,'col'=8] {'col'}, dimensions={0} | all-to-all | bytes 655360 | tf_op jit(solution)/shard_map/all_to_all | solution.py:247
  65.0 0.6 dw.1
  65.7 8.6 %all-to-all-start.3 = ((bf16[8,16,128]{2,1,0:T(8,128)(2,1)}), bf16[8,16,128]{2,1,0:T(8,128)(2,1)S(1)}, u32[]{:S(2)}, u32[]{:S(2)}) async-start(bf16[8,16,128]{2,1,0:T(8,128)(2,1)} %dw.1), calls=%async_computation.3 | async-start | bytes 65536 | tf_op jit(solution)/shard_map/all_to_all | solution.py:249
  74.2 0.0 copy-done.1
  74.2 0.0 copy-done.9
  74.2 0.0 copy-start.3
  74.3 3.1 %back.1.sent = bf16[64,32,128]{2,1,0:T(8,128)(2,1)} custom-call(s32[1,64]{1,0:T(1,128)S(1)} %copy-done.9, bf16[8,80,256]{2,1,0:T(8,128)(2,1)S(1)} %all_to_all.25.got, bf16[64,128,128]{2,1,0:T(8,128)(2,1)S(1)} %copy-done.1), custom_call_target="tpu_custom_call" | custom-call | flops 33554432 | bytes 2097152 | tf_op jit(solution)/shard_map/back/pallas_call | solution.py:252
  77.4 0.0 copy-start.11
  77.4 0.0 copy-start.13
  77.4 1.6 %all-to-all-done.3.got = bf16[8,16,128]{2,1,0:T(8,128)(2,1)S(1)} async-done(((bf16[8,16,128]{2,1,0:T(8,128)(2,1)}), bf16[8,16,128]{2,1,0:T(8,128)(2,1)S(1)}, u32[]{:S(2)}, u32[]{:S(2)}) %all-to-all-start.3) | async-done | bytes 32800 | tf_op jit(solution)/shard_map/all_to_all | solution.py:249
  79.0 0.8 attach.1
  79.7 5.3 %all-to-all-start.4 = ((bf16[64,32,128]{2,1,0:T(8,128)(2,1)}), bf16[64,32,128]{2,1,0:T(8,128)(2,1)S(1)}, u32[]{:S(2)}, u32[]{:S(2)}) async-start(bf16[64,32,128]{2,1,0:T(8,128)(2,1)} %attach.1), calls=%async_computation.4 | async-start | bytes 1048576 | tf_op jit(solution)/shard_map/all_to_all | solution.py:271
  85.0 0.0 copy-done.3
  85.0 1.2 %local_bwd.1.refs_3_ = f32[16,16,128]{2,1,0:T(8,128)S(1)} custom-call(s32[24,2]{1,0:T(8,128)S(1)} %copy.20.coord, bf16[8,80,256]{2,1,0:T(8,128)(2,1)S(1)} %all_to_all.25.got, bf16[24,128,128]{2,1,0:T(8,128)(2,1)S(1)} %copy-done.3), custom_call_target="tpu_custom_call" | custom-call | flops 12582912 | bytes 786432 | tf_op jit(solution)/shard_map/local_bwd/pallas_call | solution.py:272
  86.3 16.1 %all-to-all-done.4.refs_4_ = bf16[64,32,128]{2,1,0:T(8,128)(2,1)S(1)} async-done(((bf16[64,32,128]{2,1,0:T(8,128)(2,1)}), bf16[64,32,128]{2,1,0:T(8,128)(2,1)S(1)}, u32[]{:S(2)}, u32[]{:S(2)}) %all-to-all-start.4) | async-done | bytes 524320 | tf_op jit(solution)/shard_map/all_to_all | solution.py:271
  102.3 0.0 copy-done.11
  102.3 0.0 copy-done.13
  102.3 1.5 %final.1 = (f32[16,2048]{1,0:T(8,128)}, f32[2,16,256]{2,1,0:T(8,128)}, f32[2,128]{1,0:T(2,128)}) custom-call(s32[1]{0:T(128)S(6)} %copy.26.live.refs_0_, s32[1,64]{1,0:T(1,128)S(1)} %copy-done.11, s32[1,64]{1,0:T(1,128)S(1)} %copy-done.13, f32[16,16,128]{2,1,0:T(8,128)S(1)} %local_bwd.1.refs_3_, bf16[64,32,128]{2,1,0:T(8,128)(2,1)S(1)} %all-to-all-done.4.refs_4_), custom_call_target="tpu_custom_call" | custom-call | bytes 1048576 | tf_op jit(solution)/shard_map/final/pallas_call | solution.py:285
  (1 shorter events, 0.0 us)
Async XLA Ops:
  1.3 0.8 copy-start.4
  2.1 0.7 copy-start.10
  2.8 0.7 copy-start.12
  4.8 26.8 %all-to-all-start = ((bf16[64,16,128]{2,1,0:T(8,128)(2,1)}), bf16[64,16,128]{2,1,0:T(8,128)(2,1)S(1)}, u32[]{:S(2)}, u32[]{:S(2)}) async-start(bf16[64,16,128]{2,1,0:T(8,128)(2,1)} %pick.1), calls=%async_computation | async-start | bytes 524288 | tf_op jit(solution)/shard_map/all_to_all | solution.py:219
  20.4 1.1 %copy-start.2 = (bf16[24,128,128]{2,1,0:T(8,128)(2,1)S(1)}, bf16[24,128,128]{2,1,0:T(8,128)(2,1)}, u32[]{:S(2)}) copy-start(bf16[24,128,128]{2,1,0:T(8,128)(2,1)} %vals.3) | copy-start | bytes 2359300
  21.5 0.8 copy-start.5
  22.4 21.6 %copy-start.14 = (bf16[2,128,256]{2,1,0:T(8,128)(2,1)S(1)}, bf16[2,128,256]{2,1,0:T(8,128)(2,1)}, u32[]{:S(2)}) copy-start(bf16[2,128,256]{2,1,0:T(8,128)(2,1)} %param.19) | copy-start | bytes 393220
  22.4 21.8 %copy-start.15 = (f32[256]{0:T(256)S(1)}, f32[256]{0:T(256)}, u32[]{:S(2)}) copy-start(f32[256]{0:T(256)} %param.20) | copy-start | bytes 3076
  22.4 29.4 %copy-start.7 = (bf16[256,256]{1,0:T(8,128)(2,1)S(1)}, bf16[256,256]{1,0:T(8,128)(2,1)}, u32[]{:S(2)}) copy-start(bf16[256,256]{1,0:T(8,128)(2,1)} %cot.1) | copy-start | bytes 393220
  31.6 1.6 %copy-start = (bf16[64,128,128]{2,1,0:T(8,128)(2,1)S(1)}, bf16[64,128,128]{2,1,0:T(8,128)(2,1)}, u32[]{:S(2)}) copy-start(bf16[64,128,128]{2,1,0:T(8,128)(2,1)} %rem.3) | copy-start | bytes 6291460
  33.2 0.8 copy-start.6
  34.1 0.7 copy-start.8
  34.7 39.5 %copy-start.1 = (bf16[64,128,128]{2,1,0:T(8,128)(2,1)S(1)}, bf16[64,128,128]{2,1,0:T(8,128)(2,1)}, u32[]{:S(2)}) copy-start(bf16[64,128,128]{2,1,0:T(8,128)(2,1)} %rem.3) | copy-start | bytes 6291460
  34.7 39.5 %copy-start.9 = (s32[1,64]{1,0:T(1,128)S(1)}, s32[1,64]{1,0:T(1,128)}, u32[]{:S(2)}) copy-start(s32[1,64]{1,0:T(1,128)} %rem_dst.3) | copy-start | bytes 772
  37.2 14.6 %all-to-all-start.1 = ((bf16[8,32,256]{2,1,0:T(8,128)(2,1)}), bf16[8,32,256]{2,1,0:T(8,128)(2,1)S(1)}, u32[]{:S(2)}, u32[]{:S(2)}) async-start(bf16[8,32,256]{2,1,0:T(8,128)(2,1)} %agg.1), calls=%async_computation.1 | async-start | bytes 262144 | tf_op jit(solution)/shard_map/all_to_all | solution.py:238
  65.7 13.3 %all-to-all-start.3 = ((bf16[8,16,128]{2,1,0:T(8,128)(2,1)}), bf16[8,16,128]{2,1,0:T(8,128)(2,1)S(1)}, u32[]{:S(2)}, u32[]{:S(2)}) async-start(bf16[8,16,128]{2,1,0:T(8,128)(2,1)} %dw.1), calls=%async_computation.3 | async-start | bytes 65536 | tf_op jit(solution)/shard_map/all_to_all | solution.py:249
  74.2 10.8 %copy-start.3 = (bf16[24,128,128]{2,1,0:T(8,128)(2,1)S(1)}, bf16[24,128,128]{2,1,0:T(8,128)(2,1)}, u32[]{:S(2)}) copy-start(bf16[24,128,128]{2,1,0:T(8,128)(2,1)} %vals.3) | copy-start | bytes 2359300
  77.4 25.0 %copy-start.11 = (s32[1,64]{1,0:T(1,128)S(1)}, s32[1,64]{1,0:T(1,128)}, u32[]{:S(2)}) copy-start(s32[1,64]{1,0:T(1,128)} %refs_1_.1) | copy-start | bytes 772
  77.4 25.0 %copy-start.13 = (s32[1,64]{1,0:T(1,128)S(1)}, s32[1,64]{1,0:T(1,128)}, u32[]{:S(2)}) copy-start(s32[1,64]{1,0:T(1,128)} %refs_2_.1) | copy-start | bytes 772
  79.7 22.6 %all-to-all-start.4 = ((bf16[64,32,128]{2,1,0:T(8,128)(2,1)}), bf16[64,32,128]{2,1,0:T(8,128)(2,1)S(1)}, u32[]{:S(2)}, u32[]{:S(2)}) async-start(bf16[64,32,128]{2,1,0:T(8,128)(2,1)} %attach.1), calls=%async_computation.4 | async-start | bytes 1048576 | tf_op jit(solution)/shard_map/all_to_all | solution.py:271

commit v2 on v1

v2 whole, which is shorter than its diff:
```python
import jax
import jax.numpy as jnp
from jax import lax
from jax.experimental import pallas as pl
from jax.experimental.pallas import tpu as pltpu
from jax.sharding import PartitionSpec as P

F32 = jnp.float32
BF16 = jnp.bfloat16
NX, NZ, NCORE = 4, 8, 2
NDOM = NX * NZ * NCORE
NCOL = 8
NB = 16
W = 128
ROWS = 16
H = 256
LOC = 24
G = NX * NCORE
DW = NZ * ROWS
DB = DW + 4 * ROWS
TALL = DB + ROWS

SMEM = pl.BlockSpec(memory_space=pltpu.SMEM)
VMEM = pl.BlockSpec(memory_space=pltpu.VMEM)
ANY = pl.BlockSpec(memory_space=pl.ANY)
NT = (((1,), (1,)), ((), ()))
NN = (((1,), (0,)), ((), ()))


def dot(a, b, dims=NN):
    return lax.dot_general(a, b, dims, preferred_element_type=F32)


def call(body, out_shape, in_specs, scratch=(), flops=0, nbytes=0, name=None):
    many = isinstance(out_shape, (list, tuple))
    return pl.pallas_call(
        body,
        out_shape=out_shape,
        in_specs=in_specs,
        out_specs=[out_spec(s) for s in out_shape] if many else out_spec(out_shape),
        scratch_shapes=list(scratch),
        compiler_params=pltpu.CompilerParams(vmem_limit_bytes=24 * 2**20),
        cost_estimate=pl.CostEstimate(flops=flops, bytes_accessed=nbytes, transcendentals=0),
        name=name,
    )


def out_spec(shape):
    return SMEM if getattr(shape, "memory_space", None) == pltpu.SMEM else VMEM


def in_hbm(x):
    return pltpu.with_memory_space_constraint(x, pltpu.HBM)


def in_vmem(x):
    return pltpu.with_memory_space_constraint(x, pltpu.VMEM)


def masked_block(feats, live, b):
    node = lax.broadcasted_iota(jnp.int32, (ROWS, W), 1) + b * W
    return jnp.where(node < live, feats[:, b * W : (b + 1) * W].astype(F32), 0.0).astype(BF16)


def node_mask(live, b):
    node = lax.broadcasted_iota(jnp.int32, (ROWS, W), 1) + b * W
    return (node < live).astype(F32)


def pick_kernel(live, send_block, send_live, feats, out, xs):
    for b in range(NB):
        xs[b] = masked_block(feats, live[0], b)
    xs[NB] = jnp.zeros((ROWS, W), BF16)
    for q in range(NDOM):
        out[q] = xs[jnp.where(send_live[0, q] > 0, send_block[0, q], NB)]


def local_fwd_kernel(
    live, coord, rem_dst, send_block, send_live, feats, vals, rem, cot, local, xs, vals_here, rem_here, cot_here, places, sems
):
    copies = [
        pltpu.make_async_copy(vals, vals_here, sems.at[0]),
        pltpu.make_async_copy(rem, rem_here, sems.at[1]),
        pltpu.make_async_copy(cot, cot_here, sems.at[2]),
    ]
    for copy in copies:
        copy.start()
    for b in range(NB):
        xs[b] = masked_block(feats, live[0], b)
    local[...] = jnp.zeros_like(local)
    for q in range(NDOM):
        places[0, q] = rem_dst[0, q]
        places[1, q] = jnp.where(send_live[0, q] > 0, send_block[0, q], NB)
    for k in range(LOC):
        places[2, k] = coord[0, k]
        places[3, k] = coord[1, k]
    copies[0].wait()
    for k in range(LOC):
        local[coord[1, k]] += dot(xs[coord[0, k]], vals_here[k])
    copies[1].wait()
    copies[2].wait()


def agg_kernel(live, places, xs, arrived, local, rem, out, acc):
    acc[...] = local[...]
    for q in range(NDOM):
        acc[places[0, q]] += dot(arrived[q], rem[q])
    for c in range(NCOL):
        for j in range(2):
            b = 2 * c + j
            out[c, 0:ROWS, j * W : (j + 1) * W] = xs[b]
            out[c, ROWS : 2 * ROWS, j * W : (j + 1) * W] = (acc[b] * node_mask(live[0], b)).astype(BF16)


def dense_kernel(live, first, got, wt, w, bias, cot, hidden, out):
    node = lax.broadcasted_iota(jnp.int32, (H, H), 1) + first[0]
    mask = (node < live[0]).astype(F32)
    x = got[...].reshape(NCOL * 2 * ROWS, H)
    z = dot(wt[...], x) + bias[...]
    sig = 1.0 / (1.0 + jnp.exp(-z))
    hidden[...] = (z * sig * mask).astype(BF16)
    dz = (cot[...].astype(F32) * (sig * (1.0 + z * (1.0 - sig))) * mask).astype(BF16)
    dx = dot(w[...], dz)
    dw = dot(x, dz, NT)
    db = dot(jnp.ones((ROWS, H), BF16), dz, NT)
    mask_rows = mask[0:ROWS]
    for c in range(NCOL):
        r = c * 2 * ROWS
        out[c, 0:ROWS] = dx[r : r + ROWS].astype(BF16)
        out[c, ROWS : 2 * ROWS] = (dx[r + ROWS : r + 2 * ROWS] * mask_rows).astype(BF16)
        out[c, 2 * ROWS : 4 * ROWS] = dw[r : r + 2 * ROWS].astype(BF16)
        out[c, 4 * ROWS : 5 * ROWS] = db.astype(BF16)


def load_grad_blocks(got, gs):
    for c in range(NCOL):
        rows = got[c, ROWS : 2 * ROWS]
        gs[2 * c] = rows[:, 0:W]
        gs[2 * c + 1] = rows[:, W : 2 * W]


def back_kernel(places, got, rem, vals, out, local, gs):
    load_grad_blocks(got, gs)
    for c in range(NCOL):
        rows = got[c, 0:ROWS].astype(F32)
        local[2 * c] = rows[:, 0:W]
        local[2 * c + 1] = rows[:, W : 2 * W]
    dw = jnp.zeros((2 * ROWS, H), F32)
    db = jnp.zeros((ROWS, H), F32)
    for c in range(NCOL):
        dw = dw + got[c, 2 * ROWS : 4 * ROWS].astype(F32)
        db = db + got[c, 4 * ROWS : 5 * ROWS].astype(F32)
    dw = dw.astype(BF16)
    row = lax.broadcasted_iota(jnp.int32, (ROWS, W), 0)
    db = jnp.where(row == 0, db[:, 0:W], db[:, W : 2 * W]).astype(BF16)
    for g in range(G):
        out[g, DB:TALL] = db
        for h in range(2):
            out[g, DW + 2 * ROWS * h : DW + 2 * ROWS * (h + 1)] = dw[:, h * W : (h + 1) * W]
    for q in range(NDOM):
        x, z, core = q // (NZ * NCORE), q // NCORE % NZ, q % NCORE
        out[x * NCORE + core, z * ROWS : (z + 1) * ROWS] = dot(gs[places[0, q]], rem[q], NT).astype(BF16)
    for k in range(LOC):
        local[places[2, k]] += dot(gs[places[3, k]], vals[k], NT)


def turn_kernel(got, out):
    for g in range(G):
        for z in range(NZ):
            out[z, g * ROWS : (g + 1) * ROWS] = got[g, z * ROWS : (z + 1) * ROWS]
    total = got[0, DW:TALL].astype(F32)
    for g in range(1, G):
        total = total + got[g, DW:TALL].astype(F32)
    total = total.astype(BF16)
    for z in range(NZ):
        out[z, DW:TALL] = total


def final_kernel(factor, live, places, local, got, grad, gw, gb, acc):
    acc[0:NB] = local[...]
    for q in range(NDOM):
        x, z, core = q // (NZ * NCORE), q // NCORE % NZ, q % NCORE
        g = x * NCORE + core
        acc[places[1, q]] += got[z, g * ROWS : (g + 1) * ROWS].astype(F32)
    for b in range(NB):
        grad[:, b * W : (b + 1) * W] = acc[b] * node_mask(live[0], b)
    total = got[0, DW:TALL].astype(F32)
    for z in range(1, NZ):
        total = total + got[z, DW:TALL].astype(F32)
    total = total * factor
    for h in range(2):
        for t in range(2):
            r = 2 * ROWS * h + ROWS * t
            gw[t, :, h * W : (h + 1) * W] = total[r : r + ROWS]
    gb[...] = total[DB - DW : DB - DW + 2]


def shards(
    feats,
    part_len,
    loc_vals,
    loc_coord,
    send_block,
    send_live,
    rem_vals,
    rem_dst,
    weight,
    bias,
    cot,
):
    sds = jax.ShapeDtypeStruct
    slots = feats.shape[1]
    first = (lax.axis_index("col") * (slots // NCOL)).astype(jnp.int32).reshape(1)
    wr = weight.reshape(2, NCOL, ROWS, H).transpose(1, 0, 2, 3).reshape(NCOL * 2 * ROWS, H)
    wt = wr.T
    factor = 1.0 / float(slots * NDOM) ** 0.5
    at = lambda x, z, core: (x * NZ + z) * NCORE + core
    over_xcore = [[at(x, z, core) for x in range(NX) for core in range(NCORE)] for z in range(NZ)]
    over_z = [[at(x, z, core) for z in range(NZ)] for x in range(NX) for core in range(NCORE)]

    def swap(x, axis, groups=None):
        return lax.all_to_all(x, axis, split_axis=0, concat_axis=0, tiled=True, axis_index_groups=groups)

    picked = call(
        pick_kernel,
        sds((NDOM, ROWS, W), BF16),
        [SMEM, SMEM, SMEM, VMEM],
        [pltpu.VMEM((NB + 1, ROWS, W), BF16)],
        nbytes=320 * 1024,
        name="pick",
    )(part_len, in_hbm(send_block), in_hbm(send_live), in_hbm(feats))
    arrived = swap(picked, "dom")
    local, xs, vals_here, rem_here, cot_here, places = call(
        local_fwd_kernel,
        [
            pltpu.VMEM((NB, ROWS, W), F32),
            pltpu.VMEM((NB, ROWS, W), BF16),
            pltpu.VMEM(loc_vals.shape, BF16),
            pltpu.VMEM(rem_vals.shape, BF16),
            pltpu.VMEM(cot.shape, BF16),
            pltpu.SMEM((4, NDOM), jnp.int32),
        ],
        [SMEM, SMEM, SMEM, SMEM, SMEM, VMEM, ANY, ANY, ANY],
        [pltpu.SemaphoreType.DMA((3,))],
        flops=2 * LOC * ROWS * W * W,
        nbytes=4 * 2**20,
        name="local_fwd",
    )(
        part_len,
        in_hbm(loc_coord.T),
        in_hbm(rem_dst),
        in_hbm(send_block),
        in_hbm(send_live),
        in_hbm(feats),
        in_hbm(loc_vals),
        in_hbm(rem_vals),
        in_hbm(cot),
    )
    stacked = call(
        agg_kernel,
        sds((NCOL, 2 * ROWS, 2 * W), BF16),
        [SMEM, SMEM] + [VMEM] * 4,
        [pltpu.VMEM((NB, ROWS, W), F32)],
        flops=2 * NDOM * ROWS * W * W,
        nbytes=3 * 2**20,
        name="agg",
    )(part_len, places, xs, in_vmem(arrived), local, rem_here)
    regrouped = swap(stacked, "col")
    hidden, outgoing = call(
        dense_kernel,
        [sds((H, 2 * W), BF16), pltpu.VMEM((NCOL, 5 * ROWS, 2 * W), BF16)],
        [SMEM, SMEM] + [VMEM] * 5,
        flops=3 * 2 * H**3,
        nbytes=2**20,
        name="dense",
    )(part_len, first, in_vmem(regrouped), wt, wr, bias.reshape(H, 1), cot_here)
    returned = swap(outgoing, "col")
    terms, local_back = call(
        back_kernel,
        [pltpu.VMEM((G, TALL, W), BF16), pltpu.VMEM((NB, ROWS, W), F32)],
        [SMEM, VMEM, VMEM, VMEM],
        [pltpu.VMEM((NB, ROWS, W), BF16)],
        flops=2 * (NDOM + LOC) * ROWS * W * W,
        nbytes=4 * 2**20,
        name="back",
    )(places, in_vmem(returned), rem_here, vals_here)
    half = swap(terms, "dom", over_xcore)
    turned = call(
        turn_kernel,
        pltpu.VMEM((NZ, TALL, W), BF16),
        [VMEM],
        nbytes=2**20,
        name="turn",
    )(in_vmem(half))
    got = swap(turned, "dom", over_z)

    def final_body(*refs):
        final_kernel(factor, *refs)

    grad_feats, grad_weight, grad_bias = call(
        final_body,
        [sds((ROWS, slots), F32), sds((2, ROWS, H), F32), sds((2, W), F32)],
        [SMEM, SMEM, VMEM, VMEM],
        [pltpu.VMEM((NB + 1, ROWS, W), F32)],
        nbytes=2**20,
        name="final",
    )(part_len, places, local_back, in_vmem(got))
    return (hidden, grad_feats, grad_weight, grad_bias.reshape(H))


def solution(mesh):
    placed = (
        P("col", "dom"),
        P("dom"),
        P("dom", None, None),
        P("dom", None),
        P("dom", None),
        P("dom", None),
        P("dom", None, None),
        P("dom", None),
        P(),
        P(),
        P(None, ("dom", "col")),
    )
    return jax.shard_map(
        shards,
        mesh=mesh,
        in_specs=placed,
        out_specs=(P(None, ("dom", "col")), P("col", "dom"), P(None, "col", None), P()),
        check_vma=False,
    )
```

time: 105 us -> 95.2 us (0.907)
  blocking collectives: 12.2 us -> 45.2 us
  waiting for transfers between devices: 33.3 us -> 15.9 us
  starting transfers between devices: 35.5 us -> 21.7 us
  local copies, waits for them, and re-layouts: 8.24 us -> 1.15 us
  Pallas kernels: 13.2 us -> 9.33 us
    all_to_all x1 -> x3, blocking collectives: 12.2 us -> 45.2 us  [swap(): lax.all_to_all(x, axis, split_axis=0, concat_axis=0, tiled=True, axis_ind...]
    all_to_all x4 -> x2, waiting for transfers between devices: 33.3 us -> 15.9 us  [swap(): lax.all_to_all(x, axis, split_axis=0, concat_axis=0, tiled=True, axis_ind...]
    all_to_all x4 -> x2, starting transfers between devices: 35.5 us -> 21.7 us  [swap(): lax.all_to_all(x, axis, split_axis=0, concat_axis=0, tiled=True, axis_ind...]
    unnamed x33 -> x2, local copies, waits for them, and re-layouts: 8 us -> 0.01 us
    pallas_call x7 -> x5, Pallas kernels: 10.3 us -> 6.75 us  [the longest x1 2.73 us: shards(): call(local_fwd_kernel, [pltpu.VMEM((NB, ROWS, W), F32), pltpu.VMEM((NB, R...]
  transfers between devices with their start and end apart: 4 -> 2, of which waited for: 4 -> 2; matrix products, arithmetic and copies ran while one was open for 1% -> 1% of each run, Pallas kernels for 5% -> 3%
where the time goes in v2:
time: 95.2 us; the launch traced here: 94.6 us
  blocking collectives  45.2 us (47%)
  starting transfers between devices  21.7 us (23%)
  waiting for transfers between devices  15.9 us (17%)
  Pallas kernels  9.33 us (10%)
  between operations  1.34 us (1%)
  local copies, waits for them, and re-layouts  1.15 us (1%)
    all_to_all x3, blocking collectives, swap(): lax.all_to_all(x, axis, split_axis=0, concat_axis=0, tiled=True, axis_ind...  45.2 us
    all_to_all x2, starting transfers between devices, swap(): lax.all_to_all(x, axis, split_axis=0, concat_axis=0, tiled=True, axis_ind...  21.7 us
    all_to_all x2, waiting for transfers between devices, swap(): lax.all_to_all(x, axis, split_axis=0, concat_axis=0, tiled=True, axis_ind...  15.9 us
    pallas_call x1, Pallas kernels, shards(): call(local_fwd_kernel, [pltpu.VMEM((NB, ROWS, W), F32), pltpu.VMEM((NB, R...  2.73 us
  transfers between devices with their start and end apart: 2, of which 2 were waited for; matrix products, arithmetic and copies ran while one was open for 1% of the time, Pallas kernels for 3%

profile of v2, /device:TPU:1, one launch (start us, length us, event | category | flops | bytes accessed | tf_op | source)
XLA Modules:
  0.0 94.6 jit_solution(3177272748589965638)
XLA Ops:
  1.3 1.7 %pick.1 = bf16[64,16,128]{2,1,0:T(8,128)(2,1)} custom-call(s32[1]{0:T(128)S(6)} %copy.20.live.refs_0_, s32[1,64]{1,0:T(1,128)} %send_block.3, s32[1,64]{1,0:T(1,128)} %send_live.3, bf16[16,2048]{1,0:T(8,128)(2,1)} %feats.3), custom_call_target="tpu_custom_call" | custom-call | bytes 327680 | tf_op jit(solution)/shard_map/pick/pallas_call | solution.py:224
  2.9 14.8 %all-to-all-start = ((bf16[64,16,128]{2,1,0:T(8,128)(2,1)}), bf16[64,16,128]{2,1,0:T(8,128)(2,1)S(1)}, u32[]{:S(2)}, u32[]{:S(2)}) async-start(bf16[64,16,128]{2,1,0:T(8,128)(2,1)} %pick.1), calls=%async_computation | async-start | bytes 524288 | tf_op jit(solution)/shard_map/all_to_all | solution.py:222
  17.8 2.7 %local_fwd.1 = (f32[16,16,128]{2,1,0:T(8,128)S(1)}, bf16[16,16,128]{2,1,0:T(8,128)(2,1)S(1)}, bf16[24,128,128]{2,1,0:T(8,128)(2,1)S(1)}, bf16[64,128,128]{2,1,0:...) custom-call(s32[1]{0:T(128)S(6)} %copy.20.live.refs_0_, s32[2,24]{1,0:T(2,128)} %bitcast.13, ...), custom_call_target="tpu_custom_call" | custom-call | flops 12582912 | bytes 4194304 | tf_op jit(solution)/shard_map/local_fwd/pallas_call | solution.py:233
  20.5 0.0 copy-start
  20.5 9.2 %all-to-all-done.arrived = bf16[64,16,128]{2,1,0:T(8,128)(2,1)S(1)} async-done(((bf16[64,16,128]{2,1,0:T(8,128)(2,1)}), bf16[64,16,128]{2,1,0:T(8,128)(2,1)S(1)}, u32[]{:S(2)}, u32[]{:S(2)}) %all-to-all-start) | async-done | bytes 262176 | tf_op jit(solution)/shard_map/all_to_all | solution.py:222
  29.8 1.3 %agg.1 = bf16[8,32,256]{2,1,0:T(8,128)(2,1)} custom-call(s32[1]{0:T(128)S(6)} %copy.20.live.refs_0_, s32[4,64]{1,0:T(4,128)S(4)} %get-tuple-element.17.places.refs_1_, bf16[16,16,128]{2,1,0:T(8,128)(2,1)S(1)} %get-tuple-element.18.xs, bf16[64,16,128]{2,1,0:T(8,128)(2,1)S(1)} %all-to-all-done.arrived, f32[16,16,128]{2,1,0:T(8,128)S(1)} %get-tuple-element.19.local, ...), custom_call_target="tpu_custom_call" | custom-call | flops 33554432 | bytes 3145728 | tf_op jit(solution)/shard_map/agg/pallas_call | solution.py:259
  31.1 6.8 %all-to-all-start.1 = ((bf16[8,32,256]{2,1,0:T(8,128)(2,1)}), bf16[8,32,256]{2,1,0:T(8,128)(2,1)S(1)}, u32[]{:S(2)}, u32[]{:S(2)}) async-start(bf16[8,32,256]{2,1,0:T(8,128)(2,1)} %agg.1), calls=%async_computation.1 | async-start | bytes 262144 | tf_op jit(solution)/shard_map/all_to_all | solution.py:222
  37.9 0.9 copy.17
  38.8 0.1 copy.18.wt
  39.0 0.0 copy-done
  39.0 0.1 copy.19.bias
  39.1 6.6 %all-to-all-done.1.got = bf16[8,32,256]{2,1,0:T(8,128)(2,1)S(1)} async-done(((bf16[8,32,256]{2,1,0:T(8,128)(2,1)}), bf16[8,32,256]{2,1,0:T(8,128)(2,1)S(1)}, u32[]{:S(2)}, u32[]{:S(2)}) %all-to-all-start.1) | async-done | bytes 131104 | tf_op jit(solution)/shard_map/all_to_all | solution.py:222
  45.7 1.0 %dense.1 = (bf16[256,256]{1,0:T(8,128)(2,1)}, bf16[8,80,256]{2,1,0:T(8,128)(2,1)S(1)}) custom-call(s32[1]{0:T(128)S(6)} %copy.20.live.refs_0_, s32[1]{0:T(128)} %bitcast.first, bf16[8,32,256]{2,1,0:T(8,128)(2,1)S(1)} %all-to-all-done.1.got, bf16[256,256]{1,0:T(8,128)(2,1)S(1)} %copy.18.wt, bf16[256,256]{1,0:T(8,128)(2,1)S(1)} %bitcast.11, ...), custom_call_target="tpu_custom_call" | custom-call | flops 100663296 | bytes 1048576 | tf_op jit(solution)/shard_map/dense/pallas_call | solution.py:269
  46.8 12.2 %all_to_all.25.got = bf16[8,80,256]{2,1,0:T(8,128)(2,1)S(1)} all-to-all(bf16[8,80,256]{2,1,0:T(8,128)(2,1)S(1)} %get-tuple-element.23), channel_id=1, replica_groups=mesh['dom'=64,'col'=8] {'col'}, dimensions={0} | all-to-all | bytes 655360 | tf_op jit(solution)/shard_map/all_to_all | solution.py:222
  59.0 1.6 %back.1 = (bf16[8,208,128]{2,1,0:T(8,128)(2,1)S(1)}, f32[16,16,128]{2,1,0:T(8,128)S(1)}) custom-call(s32[4,64]{1,0:T(4,128)S(4)} %get-tuple-element.17.places.refs_1_, bf16[8,80,256]{2,1,0:T(8,128)(2,1)S(1)} %all_to_all.25.got, bf16[64,128,128]{2,1,0:T(8,128)(2,1)S(1)} %get-tuple-element.20.rem, bf16[24,128,128]{2,1,0:T(8,128)(2,1)S(1)} %get-tuple-element.24.vals), custom_call_target="tpu_custom_call" | custom-call | flops 46137344 | bytes 4194304 | tf_op jit(solution)/shard_map/back/pallas_call | solution.py:278
  60.6 16.7 %all_to_all.26.got = bf16[8,208,128]{2,1,0:T(8,128)(2,1)S(1)} all-to-all(bf16[8,208,128]{2,1,0:T(8,128)(2,1)S(1)} %get-tuple-element.26), channel_id=1, replica_groups={{0,8,128,136,256,264,384,392},{16,24,144,152,272,280,400,408},{32,40,16..., dimensions={0} | all-to-all | bytes 851968 | tf_op jit(solution)/shard_map/all_to_all | solution.py:222
  77.4 16.3 %all_to_all.27.refs_3_ = bf16[8,208,128]{2,1,0:T(8,128)(2,1)S(1)} all-to-all(bf16[8,208,128]{2,1,0:T(8,128)(2,1)S(1)} %turn.1), channel_id=1, replica_groups={{0,16,32,48,64,80,96,112},{8,24,40,56,72,88,104,120},{128,144,160,176,1..., dimensions={0} | all-to-all | bytes 851968 | tf_op jit(solution)/shard_map/all_to_all | solution.py:222
  93.7 0.9 final.1
  (1 shorter events, 0.0 us)
Async XLA Ops:
  2.9 26.8 %all-to-all-start = ((bf16[64,16,128]{2,1,0:T(8,128)(2,1)}), bf16[64,16,128]{2,1,0:T(8,128)(2,1)S(1)}, u32[]{:S(2)}, u32[]{:S(2)}) async-start(bf16[64,16,128]{2,1,0:T(8,128)(2,1)} %pick.1), calls=%async_computation | async-start | bytes 524288 | tf_op jit(solution)/shard_map/all_to_all | solution.py:222
  20.5 18.4 %copy-start = (f32[256]{0:T(256)S(1)}, f32[256]{0:T(256)}, u32[]{:S(2)}) copy-start(f32[256]{0:T(256)} %param.20) | copy-start | bytes 3076
  31.1 14.6 %all-to-all-start.1 = ((bf16[8,32,256]{2,1,0:T(8,128)(2,1)}), bf16[8,32,256]{2,1,0:T(8,128)(2,1)S(1)}, u32[]{:S(2)}, u32[]{:S(2)}) async-start(bf16[8,32,256]{2,1,0:T(8,128)(2,1)} %agg.1), calls=%async_computation.1 | async-start | bytes 262144 | tf_op jit(solution)/shard_map/all_to_all | solution.py:222

commit v3 on v2

v3 whole, which is shorter than its diff:
```python
import jax
import jax.numpy as jnp
from jax import lax
from jax.experimental import pallas as pl
from jax.experimental.pallas import tpu as pltpu
from jax.sharding import PartitionSpec as P

F32 = jnp.float32
BF16 = jnp.bfloat16
NX, NZ, NCORE = 4, 8, 2
NDOM = NX * NZ * NCORE
NCOL = 8
NB = 16
W = 128
ROWS = 16
H = 256
LOC = 24
WAYS = 4
PART = 16
G = NX * NCORE
DW = NZ * ROWS
DB = DW + 4 * ROWS
TALL = DB + ROWS
DIRECT, DAGG, DWS, DBS = 0, H, 2 * H, 4 * H
WIDE = DBS + W

SMEM = pl.BlockSpec(memory_space=pltpu.SMEM)
VMEM = pl.BlockSpec(memory_space=pltpu.VMEM)
ANY = pl.BlockSpec(memory_space=pl.ANY)
NT = (((1,), (1,)), ((), ()))
NN = (((1,), (0,)), ((), ()))


def dot(a, b, dims=NN):
    return lax.dot_general(a, b, dims, preferred_element_type=F32)


def call(body, out_shape, in_specs, scratch=(), flops=0, nbytes=0, name=None):
    many = isinstance(out_shape, (list, tuple))
    return pl.pallas_call(
        body,
        out_shape=out_shape,
        in_specs=in_specs,
        out_specs=[out_spec(s) for s in out_shape] if many else out_spec(out_shape),
        scratch_shapes=list(scratch),
        compiler_params=pltpu.CompilerParams(vmem_limit_bytes=8 * 2**20),
        cost_estimate=pl.CostEstimate(flops=flops, bytes_accessed=nbytes, transcendentals=0),
        name=name,
    )


def out_spec(shape):
    return {pltpu.SMEM: SMEM, pltpu.HBM: ANY}.get(getattr(shape, "memory_space", None), VMEM)


def in_hbm(x):
    return pltpu.with_memory_space_constraint(x, pltpu.HBM)


def in_vmem(x):
    return pltpu.with_memory_space_constraint(x, pltpu.VMEM)


def masked_block(feats, live, b):
    node = lax.broadcasted_iota(jnp.int32, (ROWS, W), 1) + b * W
    return jnp.where(node < live, feats[:, b * W : (b + 1) * W].astype(F32), 0.0).astype(BF16)


def node_mask(live, b):
    node = lax.broadcasted_iota(jnp.int32, (ROWS, W), 1) + b * W
    return (node < live).astype(F32)


def add_up(accs, b):
    total = accs[0][b]
    for acc in accs[1:]:
        total = total + acc[b]
    return total


def pick_kernel(live, send_block, send_live, feats, out, xs, buf, sems):
    for b in range(NB):
        xs[b] = masked_block(feats, live[0], b)
    xs[NB] = jnp.zeros((ROWS, W), BF16)
    copies = []
    for q in range(NDOM):
        buf[q] = xs[jnp.where(send_live[0, q] > 0, send_block[0, q], NB)]
        if q % PART == PART - 1:
            part = pl.ds(q + 1 - PART, PART)
            copies.append(pltpu.make_async_copy(buf.at[part], out.at[part], sems.at[q // PART]))
            copies[-1].start()
    for copy in copies:
        copy.wait()


def local_fwd_kernel(
    live, first, coord, rem_dst, send_block, send_live, feats, weight, bias, vals, rem, cot,
    local, xs, w_here, wt_here, bias_here, rem_here, cot_here, places, vals_here, sems,
):
    copies = [
        pltpu.make_async_copy(vals, vals_here, sems.at[0]),
        pltpu.make_async_copy(rem, rem_here, sems.at[1]),
        pltpu.make_async_copy(cot, cot_here, sems.at[2]),
    ]
    for copy in copies:
        copy.start()
    for c in range(NCOL):
        for t in range(2):
            r = (2 * c + t) * ROWS
            w_here[r : r + ROWS] = weight[t, c * ROWS : (c + 1) * ROWS]
    wt_here[...] = w_here[...].astype(F32).T.astype(BF16)
    bias_here[...] = jnp.broadcast_to(bias[...], (W, H)).T
    for b in range(NB):
        xs[b] = masked_block(feats, live[0], b)
    local[...] = jnp.zeros_like(local)
    for q in range(NDOM):
        places[0, q] = rem_dst[0, q]
        places[1, q] = jnp.where(send_live[0, q] > 0, send_block[0, q], NB)
    places[4, 0] = first[0]
    for k in range(LOC):
        places[2, k] = coord[0, k]
        places[3, k] = coord[1, k]
    copies[0].wait()
    for k in range(LOC):
        local[coord[1, k]] += dot(xs[coord[0, k]], vals_here[k])
    copies[1].wait()
    copies[2].wait()


def agg_kernel(live, places, xs, arrived, local, rem, out, *accs):
    accs[0][...] = local[...]
    for acc in accs[1:]:
        acc[...] = jnp.zeros_like(acc)
    for q in range(NDOM):
        accs[q % WAYS][places[0, q]] += dot(arrived[q], rem[q])
    for c in range(NCOL):
        for j in range(2):
            b = 2 * c + j
            out[c, 0:ROWS, j * W : (j + 1) * W] = xs[b]
            out[c, ROWS : 2 * ROWS, j * W : (j + 1) * W] = (add_up(accs, b) * node_mask(live[0], b)).astype(BF16)


def dense_kernel(live, places, got, wt, w, bias, cot, hidden, out):
    node = lax.broadcasted_iota(jnp.int32, (H, H), 1) + places[4, 0]
    mask = (node < live[0]).astype(F32)
    x = got[...].reshape(NCOL * 2 * ROWS, H)
    z = dot(wt[...], x) + jnp.concatenate([bias[...], bias[...]], axis=1)
    sig = 1.0 / (1.0 + jnp.exp(-z))
    hidden[...] = (z * sig * mask).astype(BF16)
    dz = (cot[...].astype(F32) * (sig * (1.0 + z * (1.0 - sig))) * mask).astype(BF16)
    dx = dot(w[...], dz)
    dw = dot(x, dz, NT)
    db = dot(jnp.ones((ROWS, H), BF16), dz, NT)
    mask_rows = mask[0:ROWS]
    row = lax.broadcasted_iota(jnp.int32, (ROWS, W), 0)
    db = jnp.where(row == 0, db[:, 0:W], db[:, W : 2 * W]).astype(BF16)
    for c in range(NCOL):
        r = c * 2 * ROWS
        out[c, :, DIRECT : DIRECT + H] = dx[r : r + ROWS].astype(BF16)
        out[c, :, DAGG : DAGG + H] = (dx[r + ROWS : r + 2 * ROWS] * mask_rows).astype(BF16)
        for t in range(2):
            out[c, :, DWS + t * H : DWS + (t + 1) * H] = dw[r + t * ROWS : r + (t + 1) * ROWS].astype(BF16)
        out[c, :, DBS : DBS + W] = db


def load_grad_blocks(got, gs):
    for c in range(NCOL):
        for j in range(2):
            gs[2 * c + j] = got[c, :, DAGG + j * W : DAGG + (j + 1) * W]


def back_kernel(places, got, rem, vals, hidden, out, local, hidden_out, gs, sem, *accs):
    copy = pltpu.make_async_copy(hidden, hidden_out, sem)
    copy.start()
    load_grad_blocks(got, gs)
    for c in range(NCOL):
        for j in range(2):
            accs[0][2 * c + j] = got[c, :, DIRECT + j * W : DIRECT + (j + 1) * W].astype(F32)
    for acc in accs[1:]:
        acc[...] = jnp.zeros_like(acc)
    sums = got[0, :, DWS : DBS + W].astype(F32)
    for c in range(1, NCOL):
        sums = sums + got[c, :, DWS : DBS + W].astype(F32)
    sums = sums.astype(BF16)
    for z in range(NZ):
        for i in range(5):
            r = DW + i * ROWS
            out[z, r : r + ROWS] = sums[:, i * W : (i + 1) * W]
    for q in range(NDOM):
        x, z, core = q // (NZ * NCORE), q // NCORE % NZ, q % NCORE
        g = x * NCORE + core
        out[z, g * ROWS : (g + 1) * ROWS] = dot(gs[places[0, q]], rem[q], NT).astype(BF16)
    for k in range(LOC):
        accs[k % WAYS][places[2, k]] += dot(gs[places[3, k]], vals[k], NT)
    for b in range(NB):
        local[b] = add_up(accs, b)
    copy.wait()


def turn_kernel(got, out):
    for g in range(G):
        for z in range(NZ):
            out[g, z * ROWS : (z + 1) * ROWS] = got[z, g * ROWS : (g + 1) * ROWS]
    total = got[0, DW:TALL].astype(F32)
    for z in range(1, NZ):
        total = total + got[z, DW:TALL].astype(F32)
    total = total.astype(BF16)
    for g in range(G):
        out[g, DW:TALL] = total


def final_kernel(factor, live, places, local, got, grad, gw, gb, *accs):
    accs[0][0:NB] = local[...]
    for acc in accs[1:]:
        acc[...] = jnp.zeros_like(acc)
    for q in range(NDOM):
        x, z, core = q // (NZ * NCORE), q // NCORE % NZ, q % NCORE
        g = x * NCORE + core
        accs[q % WAYS][places[1, q]] += got[g, z * ROWS : (z + 1) * ROWS].astype(F32)
    for b in range(NB):
        grad[:, b * W : (b + 1) * W] = add_up(accs, b) * node_mask(live[0], b)
    total = got[0, DW:TALL].astype(F32)
    for g in range(1, G):
        total = total + got[g, DW:TALL].astype(F32)
    total = total * factor
    for t in range(2):
        for h in range(2):
            r = (2 * t + h) * ROWS
            gw[t, :, h * W : (h + 1) * W] = total[r : r + ROWS]
    gb[...] = total[DB - DW : DB - DW + 2]


def shards(
    feats,
    part_len,
    loc_vals,
    loc_coord,
    send_block,
    send_live,
    rem_vals,
    rem_dst,
    weight,
    bias,
    cot,
):
    sds = jax.ShapeDtypeStruct
    slots = feats.shape[1]
    first = (lax.axis_index("col") * (slots // NCOL)).astype(jnp.int32).reshape(1)
    factor = 1.0 / float(slots * NDOM) ** 0.5
    at = lambda x, z, core: (x * NZ + z) * NCORE + core
    over_xcore = [[at(x, z, core) for x in range(NX) for core in range(NCORE)] for z in range(NZ)]
    over_z = [[at(x, z, core) for z in range(NZ)] for x in range(NX) for core in range(NCORE)]

    def swap(x, axis, groups=None):
        return lax.all_to_all(x, axis, split_axis=0, concat_axis=0, tiled=True, axis_index_groups=groups)

    picked = call(
        pick_kernel,
        pltpu.HBM((NDOM, ROWS, W), BF16),
        [SMEM, SMEM, SMEM, VMEM],
        [
            pltpu.VMEM((NB + 1, ROWS, W), BF16),
            pltpu.VMEM((NDOM, ROWS, W), BF16),
            pltpu.SemaphoreType.DMA((NDOM // PART,)),
        ],
        nbytes=320 * 1024,
        name="pick",
    )(part_len, in_hbm(send_block), in_hbm(send_live), in_hbm(feats))
    arrived = swap(picked, "dom")
    local, xs, w_here, wt_here, bias_here, rem_here, cot_here, places = call(
        local_fwd_kernel,
        [
            pltpu.VMEM((NB, ROWS, W), F32),
            pltpu.VMEM((NB, ROWS, W), BF16),
            pltpu.VMEM((H, H), BF16),
            pltpu.VMEM((H, H), BF16),
            pltpu.VMEM((H, W), F32),
            pltpu.VMEM(rem_vals.shape, BF16),
            pltpu.VMEM(cot.shape, BF16),
            pltpu.SMEM((5, NDOM), jnp.int32),
        ],
        [SMEM] * 6 + [VMEM] * 3 + [ANY] * 3,
        [pltpu.VMEM((LOC, W, W), BF16), pltpu.SemaphoreType.DMA((3,))],
        flops=2 * LOC * ROWS * W * W,
        nbytes=4 * 2**20,
        name="local_fwd",
    )(
        part_len,
        first,
        in_hbm(loc_coord.T),
        in_hbm(rem_dst),
        in_hbm(send_block),
        in_hbm(send_live),
        in_hbm(feats),
        in_hbm(weight),
        in_hbm(bias.reshape(1, H)),
        in_hbm(loc_vals),
        in_hbm(rem_vals),
        in_hbm(cot),
    )
    stacked = call(
        agg_kernel,
        pltpu.VMEM((NCOL, 2 * ROWS, 2 * W), BF16),
        [SMEM, SMEM] + [VMEM] * 4,
        [pltpu.VMEM((NB, ROWS, W), F32)] * WAYS,
        flops=2 * NDOM * ROWS * W * W,
        nbytes=3 * 2**20,
        name="agg",
    )(part_len, places, in_vmem(xs), in_vmem(arrived), in_vmem(local), in_vmem(rem_here))
    regrouped = swap(stacked, "col")
    hidden_here, outgoing = call(
        dense_kernel,
        [pltpu.VMEM((H, 2 * W), BF16), pltpu.VMEM((NCOL, ROWS, WIDE), BF16)],
        [SMEM, SMEM] + [VMEM] * 5,
        flops=3 * 2 * H**3,
        nbytes=2**20,
        name="dense",
    )(part_len, places, in_vmem(regrouped), in_vmem(wt_here), in_vmem(w_here), in_vmem(bias_here), in_vmem(cot_here))
    returned = swap(outgoing, "col")
    terms, local_back, hidden = call(
        back_kernel,
        [pltpu.VMEM((NZ, TALL, W), BF16), pltpu.VMEM((NB, ROWS, W), F32), pltpu.HBM((H, 2 * W), BF16)],
        [SMEM, VMEM, VMEM, VMEM, ANY],
        [pltpu.VMEM((NB, ROWS, W), BF16), pltpu.SemaphoreType.DMA] + [pltpu.VMEM((NB, ROWS, W), F32)] * WAYS,
        flops=2 * (NDOM + LOC) * ROWS * W * W,
        nbytes=4 * 2**20,
        name="back",
    )(places, in_vmem(returned), in_vmem(rem_here), in_vmem(loc_vals), in_vmem(hidden_here))
    half = swap(terms, "dom", over_z)
    turned = call(
        turn_kernel,
        pltpu.VMEM((G, TALL, W), BF16),
        [VMEM],
        nbytes=2**20,
        name="turn",
    )(in_vmem(half))
    got = swap(turned, "dom", over_xcore)

    def final_body(*refs):
        final_kernel(factor, *refs)

    grad_feats, grad_weight, grad_bias = call(
        final_body,
        [sds((ROWS, slots), F32), sds((2, ROWS, H), F32), sds((2, W), F32)],
        [SMEM, SMEM, VMEM, VMEM],
        [pltpu.VMEM((NB + 1, ROWS, W), F32)] * WAYS,
        nbytes=2**20,
        name="final",
    )(part_len, places, in_vmem(local_back), in_vmem(got))
    return (hidden, grad_feats, grad_weight, grad_bias.reshape(H))


def solution(mesh):
    placed = (
        P("col", "dom"),
        P("dom"),
        P("dom", None, None),
        P("dom", None),
        P("dom", None),
        P("dom", None),
        P("dom", None, None),
        P("dom", None),
        P(),
        P(),
        P(None, ("dom", "col")),
    )
    return jax.shard_map(
        shards,
        mesh=mesh,
        in_specs=placed,
        out_specs=(P(None, ("dom", "col")), P("col", "dom"), P(None, "col", None), P()),
        check_vma=False,
    )
```

time: 95.2 us -> 91.7 us (0.963)
  blocking collectives: 45.2 us -> 57.4 us
  starting transfers between devices: 21.7 us -> 14.8 us
  waiting for transfers between devices: 15.9 us -> 9.18 us
  local copies, waits for them, and re-layouts: 1.15 us -> 0.01 us
    all_to_all x3 -> x4, blocking collectives: 45.2 us -> 57.4 us  [swap(): lax.all_to_all(x, axis, split_axis=0, concat_axis=0, tiled=True, axis_ind...]
    all_to_all x2 -> x1, starting transfers between devices: 21.7 us -> 14.8 us  [swap(): lax.all_to_all(x, axis, split_axis=0, concat_axis=0, tiled=True, axis_ind...]
    all_to_all x2 -> x1, waiting for transfers between devices: 15.9 us -> 9.18 us  [swap(): lax.all_to_all(x, axis, split_axis=0, concat_axis=0, tiled=True, axis_ind...]
    reshape x2 -> x0, local copies, waits for them, and re-layouts: 1.05 us -> none  [the longest x1 0.91 us: shards(): weight.reshape(2, NCOL, ROWS, H).transpose(1, 0, 2, 3)]
  transfers between devices with their start and end apart: 2 -> 1, of which waited for: 2 -> 1; matrix products, arithmetic and copies ran while one was open for 1% -> 0% of each run, Pallas kernels for 3% -> 3%
where the time goes in v3:
time: 91.7 us; the launch traced here: 91.2 us
  blocking collectives  57.4 us (63%)
  starting transfers between devices  14.8 us (16%)
  waiting for transfers between devices  9.18 us (10%)
  Pallas kernels  8.51 us (9%)
  between operations  1.33 us (1%)
    all_to_all x4, blocking collectives, swap(): lax.all_to_all(x, axis, split_axis=0, concat_axis=0, tiled=True, axis_ind...  57.4 us
    all_to_all x1, starting transfers between devices, swap(): lax.all_to_all(x, axis, split_axis=0, concat_axis=0, tiled=True, axis_ind...  14.8 us
    all_to_all x1, waiting for transfers between devices, swap(): lax.all_to_all(x, axis, split_axis=0, concat_axis=0, tiled=True, axis_ind...  9.18 us
    pallas_call x1, Pallas kernels, shards(): call(local_fwd_kernel, [pltpu.VMEM((NB, ROWS, W), F32), pltpu.VMEM((NB, R...  2.8 us
    pallas_call x1, Pallas kernels, shards(): call(back_kernel, [pltpu.VMEM((NZ, TALL, W), BF16), pltpu.VMEM((NB, ROWS,...  2.01 us
  transfers between devices with their start and end apart: 1, of which 1 were waited for; matrix products, arithmetic and copies ran while one was open for 0% of the time, Pallas kernels for 3%

profile of v3, /device:TPU:1, one launch (start us, length us, event | category | flops | bytes accessed | tf_op | source)
XLA Modules:
  0.0 91.2 jit_solution(14504471364874914721)
XLA Ops:
  1.3 1.6 %pick.1 = bf16[64,16,128]{2,1,0:T(8,128)(2,1)} custom-call(s32[1]{0:T(128)S(6)} %copy.15.live.refs_0_, s32[1,64]{1,0:T(1,128)} %send_block.3, s32[1,64]{1,0:T(1,128)} %send_live.3, bf16[16,2048]{1,0:T(8,128)(2,1)} %feats.3), custom_call_target="tpu_custom_call" | custom-call | bytes 327680 | tf_op jit(solution)/shard_map/pick/pallas_call | solution.py:257
  2.9 14.8 %all-to-all-start = ((bf16[64,16,128]{2,1,0:T(8,128)(2,1)}), bf16[64,16,128]{2,1,0:T(8,128)(2,1)S(1)}, u32[]{:S(2)}, u32[]{:S(2)}) async-start(bf16[64,16,128]{2,1,0:T(8,128)(2,1)} %pick.1), calls=%async_computation | async-start | bytes 524288 | tf_op jit(solution)/shard_map/all_to_all | solution.py:255
  17.8 2.8 %local_fwd.1 = (f32[16,16,128]{2,1,0:T(8,128)S(1)}, bf16[16,16,128]{2,1,0:T(8,128)(2,1)S(1)}, bf16[256,256]{1,0:T(8,128)(2,1)S(1)}, bf16[256,256]{1,0:T(8,128)(2...) custom-call(s32[1]{0:T(128)S(6)} %copy.15.live.refs_0_, ...), custom_call_target="tpu_custom_call" | custom-call | flops 12582912 | bytes 4194304 | tf_op jit(solution)/shard_map/local_fwd/pallas_call | solution.py:270
  20.6 9.2 %all-to-all-done.arrived = bf16[64,16,128]{2,1,0:T(8,128)(2,1)S(1)} async-done(((bf16[64,16,128]{2,1,0:T(8,128)(2,1)}), bf16[64,16,128]{2,1,0:T(8,128)(2,1)S(1)}, u32[]{:S(2)}, u32[]{:S(2)}) %all-to-all-start) | async-done | bytes 262176 | tf_op jit(solution)/shard_map/all_to_all | solution.py:255
  29.8 0.0 copy-start
  29.8 0.7 agg.1
  30.5 14.4 %all_to_all.25.got = bf16[8,32,256]{2,1,0:T(8,128)(2,1)S(1)} all-to-all(bf16[8,32,256]{2,1,0:T(8,128)(2,1)S(1)} %agg.1), channel_id=1, replica_groups=mesh['dom'=64,'col'=8] {'col'}, dimensions={0} | all-to-all | bytes 262144 | tf_op jit(solution)/shard_map/all_to_all | solution.py:255
  44.9 0.5 dense.1
  45.4 12.1 %all_to_all.26.got = bf16[8,16,1152]{2,1,0:T(8,128)(2,1)S(1)} all-to-all(bf16[8,16,1152]{2,1,0:T(8,128)(2,1)S(1)} %get-tuple-element.28), channel_id=1, replica_groups=mesh['dom'=64,'col'=8] {'col'}, dimensions={0} | all-to-all | bytes 589824 | tf_op jit(solution)/shard_map/all_to_all | solution.py:255
  57.4 0.0 copy-done
  57.4 2.0 %back.1 = (bf16[8,208,128]{2,1,0:T(8,128)(2,1)S(1)}, f32[16,16,128]{2,1,0:T(8,128)S(1)}, bf16[256,256]{1,0:T(8,128)(2,1)}) custom-call(s32[5,64]{1,0:T(8,128)S(4)} %get-tuple-element.20.places.refs_1_, bf16[8,16,1152]{2,1,0:T(8,128)(2,1)S(1)} %all_to_all.26.got, bf16[64,128,128]{2,1,0:T(8,128)(2,1)S(1)} %get-tuple-element.23.rem, ...), custom_call_target="tpu_custom_call" | custom-call | flops 46137344 | bytes 4194304 | tf_op jit(solution)/shard_map/back/pallas_call | solution.py:320
  59.5 14.6 %all_to_all.27.got = bf16[8,208,128]{2,1,0:T(8,128)(2,1)S(1)} all-to-all(bf16[8,208,128]{2,1,0:T(8,128)(2,1)S(1)} %get-tuple-element.32), channel_id=1, replica_groups={{0,16,32,48,64,80,96,112},{8,24,40,56,72,88,104,120},{128,144,160,176,1..., dimensions={0} | all-to-all | bytes 851968 | tf_op jit(solution)/shard_map/all_to_all | solution.py:255
  74.1 16.3 %all_to_all.28.refs_3_ = bf16[8,208,128]{2,1,0:T(8,128)(2,1)S(1)} all-to-all(bf16[8,208,128]{2,1,0:T(8,128)(2,1)S(1)} %turn.1), channel_id=1, replica_groups={{0,8,128,136,256,264,384,392},{16,24,144,152,272,280,400,408},{32,40,16..., dimensions={0} | all-to-all | bytes 851968 | tf_op jit(solution)/shard_map/all_to_all | solution.py:255
  90.4 0.8 final.1
  (1 shorter events, 0.0 us)
Async XLA Ops:
  2.9 26.9 %all-to-all-start = ((bf16[64,16,128]{2,1,0:T(8,128)(2,1)}), bf16[64,16,128]{2,1,0:T(8,128)(2,1)S(1)}, u32[]{:S(2)}, u32[]{:S(2)}) async-start(bf16[64,16,128]{2,1,0:T(8,128)(2,1)} %pick.1), calls=%async_computation | async-start | bytes 524288 | tf_op jit(solution)/shard_map/all_to_all | solution.py:255
  29.8 27.7 %copy-start = (bf16[24,128,128]{2,1,0:T(8,128)(2,1)S(1)}, bf16[24,128,128]{2,1,0:T(8,128)(2,1)}, u32[]{:S(2)}) copy-start(bf16[24,128,128]{2,1,0:T(8,128)(2,1)} %vals.3) | copy-start | bytes 2359300

commit v4 on v3

--- a/solution.py
+++ b/solution.py
@@ -20,9 +20,9 @@
 G = NX * NCORE
 DW = NZ * ROWS
 DB = DW + 4 * ROWS
-TALL = DB + ROWS
-DIRECT, DAGG, DWS, DBS = 0, H, 2 * H, 4 * H
-WIDE = DBS + W
+TALL = DB + 8
+DIRECT, DAGG, DWS, DBS = 0, 2 * ROWS, 4 * ROWS, 8 * ROWS
+HIGH = DBS + 16
 
 SMEM = pl.BlockSpec(memory_space=pltpu.SMEM)
 VMEM = pl.BlockSpec(memory_space=pltpu.VMEM)
@@ -95,7 +95,7 @@
 
 def local_fwd_kernel(
     live, first, coord, rem_dst, send_block, send_live, feats, weight, bias, vals, rem, cot,
-    local, xs, w_here, wt_here, bias_here, rem_here, cot_here, places, vals_here, sems,
+    local, xs, w_here, wt_here, bias_here, rem_here, cot_here, places, rem_t, vals_t, vals_here, rem_buf, vals_buf, sems,
 ):
     copies = [
         pltpu.make_async_copy(vals, vals_here, sems.at[0]),
@@ -123,8 +123,19 @@
     copies[0].wait()
     for k in range(LOC):
         local[coord[1, k]] += dot(xs[coord[0, k]], vals_here[k])
+    for k in range(LOC):
+        vals_buf[k] = vals_here[k].T
     copies[1].wait()
-    copies[2].wait()
+    copies.append(pltpu.make_async_copy(vals_buf, vals_t, sems.at[3]))
+    copies[-1].start()
+    for i in range(NDOM // PART):
+        part = pl.ds(i * PART, PART)
+        for q in range(i * PART, (i + 1) * PART):
+            rem_buf[q] = rem_here[q].T
+        copies.append(pltpu.make_async_copy(rem_buf.at[part], rem_t.at[part], sems.at[4 + i]))
+        copies[-1].start()
+    for copy in copies[2:]:
+        copy.wait()
 
 
 def agg_kernel(live, places, xs, arrived, local, rem, out, *accs):
@@ -152,21 +163,35 @@
     dw = dot(x, dz, NT)
     db = dot(jnp.ones((ROWS, H), BF16), dz, NT)
     mask_rows = mask[0:ROWS]
-    row = lax.broadcasted_iota(jnp.int32, (ROWS, W), 0)
-    db = jnp.where(row == 0, db[:, 0:W], db[:, W : 2 * W]).astype(BF16)
+    row = lax.broadcasted_iota(jnp.int32, (8, W), 0)
+    db = jnp.where(row == 0, db[0:8, 0:W], db[0:8, W : 2 * W]).astype(BF16)
     for c in range(NCOL):
         r = c * 2 * ROWS
-        out[c, :, DIRECT : DIRECT + H] = dx[r : r + ROWS].astype(BF16)
-        out[c, :, DAGG : DAGG + H] = (dx[r + ROWS : r + 2 * ROWS] * mask_rows).astype(BF16)
-        for t in range(2):
-            out[c, :, DWS + t * H : DWS + (t + 1) * H] = dw[r + t * ROWS : r + (t + 1) * ROWS].astype(BF16)
-        out[c, :, DBS : DBS + W] = db
+        direct = dx[r : r + ROWS].astype(BF16)
+        dagg = (dx[r + ROWS : r + 2 * ROWS] * mask_rows).astype(BF16)
+        for j in range(2):
+            lanes = slice(j * W, (j + 1) * W)
+            out[c, DIRECT + j * ROWS : DIRECT + (j + 1) * ROWS] = direct[:, lanes]
+            out[c, DAGG + j * ROWS : DAGG + (j + 1) * ROWS] = dagg[:, lanes]
+            for t in range(2):
+                i = DWS + (2 * t + j) * ROWS
+                out[c, i : i + ROWS] = dw[r + t * ROWS : r + (t + 1) * ROWS, lanes].astype(BF16)
+        out[c, DBS:DBS + 8] = db
 
 
 def load_grad_blocks(got, gs):
     for c in range(NCOL):
         for j in range(2):
-            gs[2 * c + j] = got[c, :, DAGG + j * W : DAGG + (j + 1) * W]
+            gs[2 * c + j] = got[c, DAGG + j * ROWS : DAGG + (j + 1) * ROWS]
+
+
+def add_sums(got, start, middle, end, count):
+    dw = got[0, start:middle].astype(F32)
+    db = got[0, middle:end].astype(F32)
+    for i in range(1, count):
+        dw = dw + got[i, start:middle].astype(F32)
+        db = db + got[i, middle:end].astype(F32)
+    return dw, db
 
 
 def back_kernel(places, got, rem, vals, hidden, out, local, hidden_out, gs, sem, *accs):
@@ -175,23 +200,19 @@
     load_grad_blocks(got, gs)
     for c in range(NCOL):
         for j in range(2):
-            accs[0][2 * c + j] = got[c, :, DIRECT + j * W : DIRECT + (j + 1) * W].astype(F32)
+            accs[0][2 * c + j] = got[c, DIRECT + j * ROWS : DIRECT + (j + 1) * ROWS].astype(F32)
     for acc in accs[1:]:
         acc[...] = jnp.zeros_like(acc)
-    sums = got[0, :, DWS : DBS + W].astype(F32)
-    for c in range(1, NCOL):
-        sums = sums + got[c, :, DWS : DBS + W].astype(F32)
-    sums = sums.astype(BF16)
+    dw, db = add_sums(got, DWS, DBS, DBS + 8, NCOL)
     for z in range(NZ):
-        for i in range(5):
-            r = DW + i * ROWS
-            out[z, r : r + ROWS] = sums[:, i * W : (i + 1) * W]
+        out[z, DW:DB] = dw.astype(BF16)
+        out[z, DB:TALL] = db.astype(BF16)
     for q in range(NDOM):
         x, z, core = q // (NZ * NCORE), q // NCORE % NZ, q % NCORE
         g = x * NCORE + core
-        out[z, g * ROWS : (g + 1) * ROWS] = dot(gs[places[0, q]], rem[q], NT).astype(BF16)
+        out[z, g * ROWS : (g + 1) * ROWS] = dot(gs[places[0, q]], rem[q]).astype(BF16)
     for k in range(LOC):
-        accs[k % WAYS][places[2, k]] += dot(gs[places[3, k]], vals[k], NT)
+        accs[k % WAYS][places[2, k]] += dot(gs[places[3, k]], vals[k])
     for b in range(NB):
         local[b] = add_up(accs, b)
     copy.wait()
@@ -201,12 +222,10 @@
     for g in range(G):
         for z in range(NZ):
             out[g, z * ROWS : (z + 1) * ROWS] = got[z, g * ROWS : (g + 1) * ROWS]
-    total = got[0, DW:TALL].astype(F32)
-    for z in range(1, NZ):
-        total = total + got[z, DW:TALL].astype(F32)
-    total = total.astype(BF16)
+    dw, db = add_sums(got, DW, DB, TALL, NZ)
     for g in range(G):
-        out[g, DW:TALL] = total
+        out[g, DW:DB] = dw.astype(BF16)
+        out[g, DB:TALL] = db.astype(BF16)
 
 
 def final_kernel(factor, live, places, local, got, grad, gw, gb, *accs):
@@ -219,15 +238,13 @@
         accs[q % WAYS][places[1, q]] += got[g, z * ROWS : (z + 1) * ROWS].astype(F32)
     for b in range(NB):
         grad[:, b * W : (b + 1) * W] = add_up(accs, b) * node_mask(live[0], b)
-    total = got[0, DW:TALL].astype(F32)
-    for g in range(1, G):
-        total = total + got[g, DW:TALL].astype(F32)
-    total = total * factor
+    dw, db = add_sums(got, DW, DB, TALL, G)
+    dw = dw * factor
     for t in range(2):
         for h in range(2):
             r = (2 * t + h) * ROWS
-            gw[t, :, h * W : (h + 1) * W] = total[r : r + ROWS]
-    gb[...] = total[DB - DW : DB - DW + 2]
+            gw[t, :, h * W : (h + 1) * W] = dw[r : r + ROWS]
+    gb[...] = db[0:2] * factor
 
 
 def shards(
@@ -267,7 +284,7 @@
         name="pick",
     )(part_len, in_hbm(send_block), in_hbm(send_live), in_hbm(feats))
     arrived = swap(picked, "dom")
-    local, xs, w_here, wt_here, bias_here, rem_here, cot_here, places = call(
+    local, xs, w_here, wt_here, bias_here, rem_here, cot_here, places, rem_t, vals_t = call(
         local_fwd_kernel,
         [
             pltpu.VMEM((NB, ROWS, W), F32),
@@ -278,9 +295,16 @@
             pltpu.VMEM(rem_vals.shape, BF16),
             pltpu.VMEM(cot.shape, BF16),
             pltpu.SMEM((5, NDOM), jnp.int32),
+            pltpu.HBM(rem_vals.shape, BF16),
+            pltpu.HBM(loc_vals.shape, BF16),
         ],
         [SMEM] * 6 + [VMEM] * 3 + [ANY] * 3,
-        [pltpu.VMEM((LOC, W, W), BF16), pltpu.SemaphoreType.DMA((3,))],
+        [
+            pltpu.VMEM((LOC, W, W), BF16),
+            pltpu.VMEM((NDOM, W, W), BF16),
+            pltpu.VMEM((LOC, W, W), BF16),
+            pltpu.SemaphoreType.DMA((4 + NDOM // PART,)),
+        ],
         flops=2 * LOC * ROWS * W * W,
         nbytes=4 * 2**20,
         name="local_fwd",
@@ -310,7 +334,7 @@
     regrouped = swap(stacked, "col")
     hidden_here, outgoing = call(
         dense_kernel,
-        [pltpu.VMEM((H, 2 * W), BF16), pltpu.VMEM((NCOL, ROWS, WIDE), BF16)],
+        [pltpu.VMEM((H, 2 * W), BF16), pltpu.VMEM((NCOL, HIGH, W), BF16)],
         [SMEM, SMEM] + [VMEM] * 5,
         flops=3 * 2 * H**3,
         nbytes=2**20,
@@ -325,7 +349,7 @@
         flops=2 * (NDOM + LOC) * ROWS * W * W,
         nbytes=4 * 2**20,
         name="back",
-    )(places, in_vmem(returned), in_vmem(rem_here), in_vmem(loc_vals), in_vmem(hidden_here))
+    )(places, in_vmem(returned), in_vmem(rem_t), in_vmem(vals_t), in_vmem(hidden_here))
     half = swap(terms, "dom", over_z)
     turned = call(
         turn_kernel,

time: 91.7 us -> 90.9 us (level)
  waiting for transfers between devices: 9.18 us -> 7.54 us
  Pallas kernels: 8.51 us -> 9.62 us
    all_to_all x1, waiting for transfers between devices: 9.18 us -> 7.54 us  [swap(): lax.all_to_all(x, axis, split_axis=0, concat_axis=0, tiled=True, axis_ind...]
    pallas_call x1, Pallas kernels: 2.8 us -> 4.45 us  [shards(): call(local_fwd_kernel, [pltpu.VMEM((NB, ROWS, W), F32), pltpu.VMEM((NB, R...]
  transfers between devices with their start and end apart: 1 -> 1, of which waited for: 1 -> 1; matrix products, arithmetic and copies ran while one was open for 0% -> 0% of each run, Pallas kernels for 3% -> 5%
where the time goes in v4:
time: 90.9 us; the launch traced here: 90.5 us
  blocking collectives  57.2 us (63%)
  starting transfers between devices  14.8 us (16%)
  Pallas kernels  9.62 us (11%)
  waiting for transfers between devices  7.54 us (8%)
  between operations  1.34 us (1%)
    all_to_all x4, blocking collectives, swap(): lax.all_to_all(x, axis, split_axis=0, concat_axis=0, tiled=True, axis_ind...  57.2 us
    all_to_all x1, starting transfers between devices, swap(): lax.all_to_all(x, axis, split_axis=0, concat_axis=0, tiled=True, axis_ind...  14.8 us
    all_to_all x1, waiting for transfers between devices, swap(): lax.all_to_all(x, axis, split_axis=0, concat_axis=0, tiled=True, axis_ind...  7.54 us
    pallas_call x1, Pallas kernels, shards(): call(local_fwd_kernel, [pltpu.VMEM((NB, ROWS, W), F32), pltpu.VMEM((NB, R...  4.45 us
  transfers between devices with their start and end apart: 1, of which 1 were waited for; matrix products, arithmetic and copies ran while one was open for 0% of the time, Pallas kernels for 5%

profile of v4, /device:TPU:1, one launch (start us, length us, event | category | flops | bytes accessed | tf_op | source)
XLA Modules:
  0.0 90.5 jit_solution(7414961499815370983)
XLA Ops:
  1.3 1.6 %pick.1 = bf16[64,16,128]{2,1,0:T(8,128)(2,1)} custom-call(s32[1]{0:T(128)S(6)} %copy.15.live.refs_0_, s32[1,64]{1,0:T(1,128)} %send_block.3, s32[1,64]{1,0:T(1,128)} %send_live.3, bf16[16,2048]{1,0:T(8,128)(2,1)} %feats.3), custom_call_target="tpu_custom_call" | custom-call | bytes 327680 | tf_op jit(solution)/shard_map/pick/pallas_call | solution.py:274
  2.9 14.8 %all-to-all-start = ((bf16[64,16,128]{2,1,0:T(8,128)(2,1)}), bf16[64,16,128]{2,1,0:T(8,128)(2,1)S(1)}, u32[]{:S(2)}, u32[]{:S(2)}) async-start(bf16[64,16,128]{2,1,0:T(8,128)(2,1)} %pick.1), calls=%async_computation | async-start | bytes 524288 | tf_op jit(solution)/shard_map/all_to_all | solution.py:272
  17.8 4.5 %local_fwd.1 = (f32[16,16,128]{2,1,0:T(8,128)S(1)}, bf16[16,16,128]{2,1,0:T(8,128)(2,1)S(1)}, bf16[256,256]{1,0:T(8,128)(2,1)S(1)}, bf16[256,256]{1,0:T(8,128)(2...) custom-call(s32[1]{0:T(128)S(6)} %copy.15.live.refs_0_, ...), custom_call_target="tpu_custom_call" | custom-call | flops 12582912 | bytes 4194304 | tf_op jit(solution)/shard_map/local_fwd/pallas_call | solution.py:287
  22.2 7.5 %all-to-all-done.arrived = bf16[64,16,128]{2,1,0:T(8,128)(2,1)S(1)} async-done(((bf16[64,16,128]{2,1,0:T(8,128)(2,1)}), bf16[64,16,128]{2,1,0:T(8,128)(2,1)S(1)}, u32[]{:S(2)}, u32[]{:S(2)}) %all-to-all-start) | async-done | bytes 262176 | tf_op jit(solution)/shard_map/all_to_all | solution.py:272
  29.8 0.0 copy-start
  29.8 0.0 copy-start.1
  29.8 0.7 agg.1
  30.5 14.5 %all_to_all.25.got = bf16[8,32,256]{2,1,0:T(8,128)(2,1)S(1)} all-to-all(bf16[8,32,256]{2,1,0:T(8,128)(2,1)S(1)} %agg.1), channel_id=1, replica_groups=mesh['dom'=64,'col'=8] {'col'}, dimensions={0} | all-to-all | bytes 262144 | tf_op jit(solution)/shard_map/all_to_all | solution.py:272
  45.0 0.5 dense.1
  45.5 12.0 %all_to_all.26.got = bf16[8,144,128]{2,1,0:T(8,128)(2,1)S(1)} all-to-all(bf16[8,144,128]{2,1,0:T(8,128)(2,1)S(1)} %get-tuple-element.30), channel_id=1, replica_groups=mesh['dom'=64,'col'=8] {'col'}, dimensions={0} | all-to-all | bytes 589824 | tf_op jit(solution)/shard_map/all_to_all | solution.py:272
  57.6 0.0 copy-done
  57.6 0.0 copy-done.1
  57.6 1.5 %back.1 = (bf16[8,200,128]{2,1,0:T(8,128)(2,1)S(1)}, f32[16,16,128]{2,1,0:T(8,128)S(1)}, bf16[256,256]{1,0:T(8,128)(2,1)}) custom-call(s32[5,64]{1,0:T(8,128)S(4)} %get-tuple-element.22.places.refs_1_, bf16[8,144,128]{2,1,0:T(8,128)(2,1)S(1)} %all_to_all.26.got, bf16[64,128,128]{2,1,0:T(8,128)(2,1)S(1)} %copy-done, bf16[24,128,128]{2,1,0:T(8,128)(2,1)S(1)} %copy-done.1, ...), custom_call_target="tpu_custom_call" | custom-call | flops 46137344 | bytes 4194304 | tf_op jit(solution)/shard_map/back/pallas_call | solution.py:344
  59.0 14.5 %all_to_all.27.got = bf16[8,200,128]{2,1,0:T(8,128)(2,1)S(1)} all-to-all(bf16[8,200,128]{2,1,0:T(8,128)(2,1)S(1)} %get-tuple-element.36), channel_id=1, replica_groups={{0,16,32,48,64,80,96,112},{8,24,40,56,72,88,104,120},{128,144,160,176,1..., dimensions={0} | all-to-all | bytes 819200 | tf_op jit(solution)/shard_map/all_to_all | solution.py:272
  73.6 16.1 %all_to_all.28.refs_3_ = bf16[8,200,128]{2,1,0:T(8,128)(2,1)S(1)} all-to-all(bf16[8,200,128]{2,1,0:T(8,128)(2,1)S(1)} %turn.1), channel_id=1, replica_groups={{0,8,128,136,256,264,384,392},{16,24,144,152,272,280,400,408},{32,40,16..., dimensions={0} | all-to-all | bytes 819200 | tf_op jit(solution)/shard_map/all_to_all | solution.py:272
  89.7 0.8 final.1
  (1 shorter events, 0.0 us)
Async XLA Ops:
  2.9 26.9 %all-to-all-start = ((bf16[64,16,128]{2,1,0:T(8,128)(2,1)}), bf16[64,16,128]{2,1,0:T(8,128)(2,1)S(1)}, u32[]{:S(2)}, u32[]{:S(2)}) async-start(bf16[64,16,128]{2,1,0:T(8,128)(2,1)} %pick.1), calls=%async_computation | async-start | bytes 524288 | tf_op jit(solution)/shard_map/all_to_all | solution.py:272
  29.8 27.8 %copy-start = (bf16[64,128,128]{2,1,0:T(8,128)(2,1)S(1)}, bf16[64,128,128]{2,1,0:T(8,128)(2,1)}, u32[]{:S(2)}) copy-start(bf16[64,128,128]{2,1,0:T(8,128)(2,1)} %get-tuple-element.31.rem) | copy-start | bytes 6291460
  29.8 27.8 %copy-start.1 = (bf16[24,128,128]{2,1,0:T(8,128)(2,1)S(1)}, bf16[24,128,128]{2,1,0:T(8,128)(2,1)}, u32[]{:S(2)}) copy-start(bf16[24,128,128]{2,1,0:T(8,128)(2,1)} %get-tuple-element.32.vals) | copy-start | bytes 2359300

commit v5 on v4

--- a/solution.py
+++ b/solution.py
@@ -197,6 +197,15 @@
 def back_kernel(places, got, rem, vals, hidden, out, local, hidden_out, gs, sem, *accs):
     copy = pltpu.make_async_copy(hidden, hidden_out, sem)
     copy.start()
+
+    @pl.when(places[0, 0] >= 0)
+    def _():
+        back_body(places, got, rem, vals, out, local, gs, accs)
+
+    copy.wait()
+
+
+def back_body(places, got, rem, vals, out, local, gs, accs):
     load_grad_blocks(got, gs)
     for c in range(NCOL):
         for j in range(2):
@@ -215,7 +224,6 @@
         accs[k % WAYS][places[2, k]] += dot(gs[places[3, k]], vals[k])
     for b in range(NB):
         local[b] = add_up(accs, b)
-    copy.wait()
 
 
 def turn_kernel(got, out):

time: 90.9 us -> 90.4 us (level)
  no operation moved by 1% of the time
where the time goes in v5:
time: 90.4 us; the launch traced here: 89.9 us
  blocking collectives  57.2 us (63%)
  starting transfers between devices  14.8 us (16%)
  Pallas kernels  9.06 us (10%)
  waiting for transfers between devices  7.54 us (8%)
  between operations  1.34 us (1%)
    all_to_all x4, blocking collectives, swap(): lax.all_to_all(x, axis, split_axis=0, concat_axis=0, tiled=True, axis_ind...  57.2 us
    all_to_all x1, starting transfers between devices, swap(): lax.all_to_all(x, axis, split_axis=0, concat_axis=0, tiled=True, axis_ind...  14.8 us
    all_to_all x1, waiting for transfers between devices, swap(): lax.all_to_all(x, axis, split_axis=0, concat_axis=0, tiled=True, axis_ind...  7.54 us
    pallas_call x1, Pallas kernels, shards(): call(local_fwd_kernel, [pltpu.VMEM((NB, ROWS, W), F32), pltpu.VMEM((NB, R...  4.45 us
  transfers between devices with their start and end apart: 1, of which 1 were waited for; matrix products, arithmetic and copies ran while one was open for 0% of the time, Pallas kernels for 5%

profile of v5, /device:TPU:1, one launch (start us, length us, event | category | flops | bytes accessed | tf_op | source)
XLA Modules:
  0.0 89.9 jit_solution(1786683789874113469)
XLA Ops:
  1.3 1.6 %pick.1 = bf16[64,16,128]{2,1,0:T(8,128)(2,1)} custom-call(s32[1]{0:T(128)S(6)} %copy.15.live.refs_0_, s32[1,64]{1,0:T(1,128)} %send_block.3, s32[1,64]{1,0:T(1,128)} %send_live.3, bf16[16,2048]{1,0:T(8,128)(2,1)} %feats.3), custom_call_target="tpu_custom_call" | custom-call | bytes 327680 | tf_op jit(solution)/shard_map/pick/pallas_call | solution.py:282
  2.9 14.8 %all-to-all-start = ((bf16[64,16,128]{2,1,0:T(8,128)(2,1)}), bf16[64,16,128]{2,1,0:T(8,128)(2,1)S(1)}, u32[]{:S(2)}, u32[]{:S(2)}) async-start(bf16[64,16,128]{2,1,0:T(8,128)(2,1)} %pick.1), calls=%async_computation | async-start | bytes 524288 | tf_op jit(solution)/shard_map/all_to_all | solution.py:280
  17.8 4.5 %local_fwd.1 = (f32[16,16,128]{2,1,0:T(8,128)S(1)}, bf16[16,16,128]{2,1,0:T(8,128)(2,1)S(1)}, bf16[256,256]{1,0:T(8,128)(2,1)S(1)}, bf16[256,256]{1,0:T(8,128)(2...) custom-call(s32[1]{0:T(128)S(6)} %copy.15.live.refs_0_, ...), custom_call_target="tpu_custom_call" | custom-call | flops 12582912 | bytes 4194304 | tf_op jit(solution)/shard_map/local_fwd/pallas_call | solution.py:295
  22.2 7.5 %all-to-all-done.arrived = bf16[64,16,128]{2,1,0:T(8,128)(2,1)S(1)} async-done(((bf16[64,16,128]{2,1,0:T(8,128)(2,1)}), bf16[64,16,128]{2,1,0:T(8,128)(2,1)S(1)}, u32[]{:S(2)}, u32[]{:S(2)}) %all-to-all-start) | async-done | bytes 262176 | tf_op jit(solution)/shard_map/all_to_all | solution.py:280
  29.8 0.0 copy-start
  29.8 0.0 copy-start.1
  29.8 0.7 agg.1
  30.5 14.5 %all_to_all.25.got = bf16[8,32,256]{2,1,0:T(8,128)(2,1)S(1)} all-to-all(bf16[8,32,256]{2,1,0:T(8,128)(2,1)S(1)} %agg.1), channel_id=1, replica_groups=mesh['dom'=64,'col'=8] {'col'}, dimensions={0} | all-to-all | bytes 262144 | tf_op jit(solution)/shard_map/all_to_all | solution.py:280
  45.0 0.5 dense.1
  45.5 12.0 %all_to_all.26.got = bf16[8,144,128]{2,1,0:T(8,128)(2,1)S(1)} all-to-all(bf16[8,144,128]{2,1,0:T(8,128)(2,1)S(1)} %get-tuple-element.30), channel_id=1, replica_groups=mesh['dom'=64,'col'=8] {'col'}, dimensions={0} | all-to-all | bytes 589824 | tf_op jit(solution)/shard_map/all_to_all | solution.py:280
  57.6 0.0 copy-done
  57.6 0.0 copy-done.1
  57.6 0.9 %back.1 = (bf16[8,200,128]{2,1,0:T(8,128)(2,1)S(1)}, f32[16,16,128]{2,1,0:T(8,128)S(1)}, bf16[256,256]{1,0:T(8,128)(2,1)}) custom-call(s32[5,64]{1,0:T(8,128)S(4)} %get-tuple-element.22.places.refs_1_, bf16[8,144,128]{2,1,0:T(8,128)(2,1)S(1)} %all_to_all.26.got, bf16[64,128,128]{2,1,0:T(8,128)(2,1)S(1)} %copy-done, bf16[24,128,128]{2,1,0:T(8,128)(2,1)S(1)} %copy-done.1, ...), custom_call_target="tpu_custom_call" | custom-call | flops 46137344 | bytes 4194304 | tf_op jit(solution)/shard_map/back/pallas_call | solution.py:352
  58.5 14.5 %all_to_all.27.got = bf16[8,200,128]{2,1,0:T(8,128)(2,1)S(1)} all-to-all(bf16[8,200,128]{2,1,0:T(8,128)(2,1)S(1)} %get-tuple-element.36), channel_id=1, replica_groups={{0,16,32,48,64,80,96,112},{8,24,40,56,72,88,104,120},{128,144,160,176,1..., dimensions={0} | all-to-all | bytes 819200 | tf_op jit(solution)/shard_map/all_to_all | solution.py:280
  73.0 16.1 %all_to_all.28.refs_3_ = bf16[8,200,128]{2,1,0:T(8,128)(2,1)S(1)} all-to-all(bf16[8,200,128]{2,1,0:T(8,128)(2,1)S(1)} %turn.1), channel_id=1, replica_groups={{0,8,128,136,256,264,384,392},{16,24,144,152,272,280,400,408},{32,40,16..., dimensions={0} | all-to-all | bytes 819200 | tf_op jit(solution)/shard_map/all_to_all | solution.py:280
  89.1 0.8 final.1
  (1 shorter events, 0.0 us)
Async XLA Ops:
  2.9 26.9 %all-to-all-start = ((bf16[64,16,128]{2,1,0:T(8,128)(2,1)}), bf16[64,16,128]{2,1,0:T(8,128)(2,1)S(1)}, u32[]{:S(2)}, u32[]{:S(2)}) async-start(bf16[64,16,128]{2,1,0:T(8,128)(2,1)} %pick.1), calls=%async_computation | async-start | bytes 524288 | tf_op jit(solution)/shard_map/all_to_all | solution.py:280
  29.8 27.8 %copy-start = (bf16[64,128,128]{2,1,0:T(8,128)(2,1)S(1)}, bf16[64,128,128]{2,1,0:T(8,128)(2,1)}, u32[]{:S(2)}) copy-start(bf16[64,128,128]{2,1,0:T(8,128)(2,1)} %get-tuple-element.31.rem) | copy-start | bytes 6291460
  29.8 27.8 %copy-start.1 = (bf16[24,128,128]{2,1,0:T(8,128)(2,1)S(1)}, bf16[24,128,128]{2,1,0:T(8,128)(2,1)}, u32[]{:S(2)}) copy-start(bf16[24,128,128]{2,1,0:T(8,128)(2,1)} %get-tuple-element.32.vals) | copy-start | bytes 2359300

commit v6 on v5

--- a/solution.py
+++ b/solution.py
@@ -22,7 +22,7 @@
 DB = DW + 4 * ROWS
 TALL = DB + 8
 DIRECT, DAGG, DWS, DBS = 0, 2 * ROWS, 4 * ROWS, 8 * ROWS
-HIGH = DBS + 16
+HIGH = DBS + 8
 
 SMEM = pl.BlockSpec(memory_space=pltpu.SMEM)
 VMEM = pl.BlockSpec(memory_space=pltpu.VMEM)
@@ -348,7 +348,7 @@
         nbytes=2**20,
         name="dense",
     )(part_len, places, in_vmem(regrouped), in_vmem(wt_here), in_vmem(w_here), in_vmem(bias_here), in_vmem(cot_here))
-    returned = swap(outgoing, "col")
+    returned = swap(outgoing.reshape(NCOL, HIGH // 8, 8, W), "col").reshape(NCOL, HIGH, W)
     terms, local_back, hidden = call(
         back_kernel,
         [pltpu.VMEM((NZ, TALL, W), BF16), pltpu.VMEM((NB, ROWS, W), F32), pltpu.HBM((H, 2 * W), BF16)],

time: 90.4 us -> 90.1 us (level)
  no operation moved by 1% of the time
where the time goes in v6:
time: 90.1 us; the launch traced here: 89.7 us
  blocking collectives  56.9 us (63%)
  starting transfers between devices  14.8 us (16%)
  Pallas kernels  9.07 us (10%)
  waiting for transfers between devices  7.54 us (8%)
  between operations  1.34 us (1%)
    all_to_all x4, blocking collectives, swap(): lax.all_to_all(x, axis, split_axis=0, concat_axis=0, tiled=True, axis_ind...  56.9 us
    all_to_all x1, starting transfers between devices, swap(): lax.all_to_all(x, axis, split_axis=0, concat_axis=0, tiled=True, axis_ind...  14.8 us
    all_to_all x1, waiting for transfers between devices, swap(): lax.all_to_all(x, axis, split_axis=0, concat_axis=0, tiled=True, axis_ind...  7.54 us
    pallas_call x1, Pallas kernels, shards(): call(local_fwd_kernel, [pltpu.VMEM((NB, ROWS, W), F32), pltpu.VMEM((NB, R...  4.45 us
  transfers between devices with their start and end apart: 1, of which 1 were waited for; matrix products, arithmetic and copies ran while one was open for 0% of the time, Pallas kernels for 5%

profile of v6, /device:TPU:1, one launch (start us, length us, event | category | flops | bytes accessed | tf_op | source)
XLA Modules:
  0.0 89.7 jit_solution(6774865565166425857)
XLA Ops:
  1.3 1.6 %pick.1 = bf16[64,16,128]{2,1,0:T(8,128)(2,1)} custom-call(s32[1]{0:T(128)S(6)} %copy.15.live.refs_0_, s32[1,64]{1,0:T(1,128)} %send_block.3, s32[1,64]{1,0:T(1,128)} %send_live.3, bf16[16,2048]{1,0:T(8,128)(2,1)} %feats.3), custom_call_target="tpu_custom_call" | custom-call | bytes 327680 | tf_op jit(solution)/shard_map/pick/pallas_call | solution.py:282
  2.9 14.8 %all-to-all-start = ((bf16[64,16,128]{2,1,0:T(8,128)(2,1)}), bf16[64,16,128]{2,1,0:T(8,128)(2,1)S(1)}, u32[]{:S(2)}, u32[]{:S(2)}) async-start(bf16[64,16,128]{2,1,0:T(8,128)(2,1)} %pick.1), calls=%async_computation | async-start | bytes 524288 | tf_op jit(solution)/shard_map/all_to_all | solution.py:280
  17.8 4.5 %local_fwd.1 = (f32[16,16,128]{2,1,0:T(8,128)S(1)}, bf16[16,16,128]{2,1,0:T(8,128)(2,1)S(1)}, bf16[256,256]{1,0:T(8,128)(2,1)S(1)}, bf16[256,256]{1,0:T(8,128)(2...) custom-call(s32[1]{0:T(128)S(6)} %copy.15.live.refs_0_, ...), custom_call_target="tpu_custom_call" | custom-call | flops 12582912 | bytes 4194304 | tf_op jit(solution)/shard_map/local_fwd/pallas_call | solution.py:295
  22.2 7.5 %all-to-all-done.arrived = bf16[64,16,128]{2,1,0:T(8,128)(2,1)S(1)} async-done(((bf16[64,16,128]{2,1,0:T(8,128)(2,1)}), bf16[64,16,128]{2,1,0:T(8,128)(2,1)S(1)}, u32[]{:S(2)}, u32[]{:S(2)}) %all-to-all-start) | async-done | bytes 262176 | tf_op jit(solution)/shard_map/all_to_all | solution.py:280
  29.8 0.0 copy-start
  29.8 0.0 copy-start.1
  29.8 0.7 agg.1
  30.5 14.5 %all_to_all.25.got = bf16[8,32,256]{2,1,0:T(8,128)(2,1)S(1)} all-to-all(bf16[8,32,256]{2,1,0:T(8,128)(2,1)S(1)} %agg.1), channel_id=1, replica_groups=mesh['dom'=64,'col'=8] {'col'}, dimensions={0} | all-to-all | bytes 262144 | tf_op jit(solution)/shard_map/all_to_all | solution.py:280
  45.0 0.5 dense.1
  45.5 11.9 %all_to_all.26 = bf16[8,17,8,128]{3,2,1,0:T(8,128)(2,1)S(1)} all-to-all(bf16[8,17,8,128]{3,2,1,0:T(8,128)(2,1)S(1)} %bitcast.7), channel_id=1, replica_groups=mesh['dom'=64,'col'=8] {'col'}, dimensions={0} | all-to-all | bytes 557056 | tf_op jit(solution)/shard_map/all_to_all | solution.py:280
  57.5 0.0 copy-done
  57.5 0.0 copy-done.1
  57.5 0.9 %back.1 = (bf16[8,200,128]{2,1,0:T(8,128)(2,1)S(1)}, f32[16,16,128]{2,1,0:T(8,128)S(1)}, bf16[256,256]{1,0:T(8,128)(2,1)}) custom-call(s32[5,64]{1,0:T(8,128)S(4)} %get-tuple-element.22.places.refs_1_, bf16[8,136,128]{2,1,0:T(8,128)(2,1)S(1)} %bitcast.6, bf16[64,128,128]{2,1,0:T(8,128)(2,1)S(1)} %copy-done, bf16[24,128,128]{2,1,0:T(8,128)(2,1)S(1)} %copy-done.1, ...), custom_call_target="tpu_custom_call" | custom-call | flops 46137344 | bytes 4194304 | tf_op jit(solution)/shard_map/back/pallas_call | solution.py:352
  58.4 14.5 %all_to_all.27.got = bf16[8,200,128]{2,1,0:T(8,128)(2,1)S(1)} all-to-all(bf16[8,200,128]{2,1,0:T(8,128)(2,1)S(1)} %get-tuple-element.36), channel_id=1, replica_groups={{0,16,32,48,64,80,96,112},{8,24,40,56,72,88,104,120},{128,144,160,176,1..., dimensions={0} | all-to-all | bytes 819200 | tf_op jit(solution)/shard_map/all_to_all | solution.py:280
  72.9 15.9 %all_to_all.28.refs_3_ = bf16[8,200,128]{2,1,0:T(8,128)(2,1)S(1)} all-to-all(bf16[8,200,128]{2,1,0:T(8,128)(2,1)S(1)} %turn.1), channel_id=1, replica_groups={{0,8,128,136,256,264,384,392},{16,24,144,152,272,280,400,408},{32,40,16..., dimensions={0} | all-to-all | bytes 819200 | tf_op jit(solution)/shard_map/all_to_all | solution.py:280
  88.9 0.8 final.1
  (1 shorter events, 0.0 us)
Async XLA Ops:
  2.9 26.9 %all-to-all-start = ((bf16[64,16,128]{2,1,0:T(8,128)(2,1)}), bf16[64,16,128]{2,1,0:T(8,128)(2,1)S(1)}, u32[]{:S(2)}, u32[]{:S(2)}) async-start(bf16[64,16,128]{2,1,0:T(8,128)(2,1)} %pick.1), calls=%async_computation | async-start | bytes 524288 | tf_op jit(solution)/shard_map/all_to_all | solution.py:280
  29.8 27.7 %copy-start = (bf16[64,128,128]{2,1,0:T(8,128)(2,1)S(1)}, bf16[64,128,128]{2,1,0:T(8,128)(2,1)}, u32[]{:S(2)}) copy-start(bf16[64,128,128]{2,1,0:T(8,128)(2,1)} %get-tuple-element.31.rem) | copy-start | bytes 6291460
  29.8 27.7 %copy-start.1 = (bf16[24,128,128]{2,1,0:T(8,128)(2,1)S(1)}, bf16[24,128,128]{2,1,0:T(8,128)(2,1)}, u32[]{:S(2)}) copy-start(bf16[24,128,128]{2,1,0:T(8,128)(2,1)} %get-tuple-element.32.vals) | copy-start | bytes 2359300

commit v7 on v6

--- a/solution.py
+++ b/solution.py
@@ -291,7 +291,7 @@
         nbytes=320 * 1024,
         name="pick",
     )(part_len, in_hbm(send_block), in_hbm(send_live), in_hbm(feats))
-    arrived = swap(picked, "dom")
+    arrived = swap(picked.reshape(NDOM, 2, 8, W), "dom").reshape(NDOM, ROWS, W)
     local, xs, w_here, wt_here, bias_here, rem_here, cot_here, places, rem_t, vals_t = call(
         local_fwd_kernel,
         [
@@ -358,7 +358,7 @@
         nbytes=4 * 2**20,
         name="back",
     )(places, in_vmem(returned), in_vmem(rem_t), in_vmem(vals_t), in_vmem(hidden_here))
-    half = swap(terms, "dom", over_z)
+    half = swap(terms.reshape(NZ, TALL // 8, 8, W), "dom", over_z).reshape(NZ, TALL, W)
     turned = call(
         turn_kernel,
         pltpu.VMEM((G, TALL, W), BF16),
@@ -366,7 +366,7 @@
         nbytes=2**20,
         name="turn",
     )(in_vmem(half))
-    got = swap(turned, "dom", over_xcore)
+    got = swap(turned.reshape(G, TALL // 8, 8, W), "dom", over_xcore).reshape(G, TALL, W)
 
     def final_body(*refs):
         final_kernel(factor, *refs)

time: 90.1 us -> 90.1 us (level)
  no operation moved by 1% of the time
where the time goes in v7:
time: 90.1 us; the launch traced here: 89.7 us
  blocking collectives  56.9 us (63%)
  starting transfers between devices  14.8 us (16%)
  Pallas kernels  9.07 us (10%)
  waiting for transfers between devices  7.54 us (8%)
  between operations  1.34 us (1%)
    all_to_all x4, blocking collectives, swap(): lax.all_to_all(x, axis, split_axis=0, concat_axis=0, tiled=True, axis_ind...  56.9 us
    all_to_all x1, starting transfers between devices, swap(): lax.all_to_all(x, axis, split_axis=0, concat_axis=0, tiled=True, axis_ind...  14.8 us
    all_to_all x1, waiting for transfers between devices, swap(): lax.all_to_all(x, axis, split_axis=0, concat_axis=0, tiled=True, axis_ind...  7.54 us
    pallas_call x1, Pallas kernels, shards(): call(local_fwd_kernel, [pltpu.VMEM((NB, ROWS, W), F32), pltpu.VMEM((NB, R...  4.45 us
  transfers between devices with their start and end apart: 1, of which 1 were waited for; matrix products, arithmetic and copies ran while one was open for 0% of the time, Pallas kernels for 5%

profile of v7, /device:TPU:1, one launch (start us, length us, event | category | flops | bytes accessed | tf_op | source)
XLA Modules:
  0.0 89.7 jit_solution(16294609367521530544)
XLA Ops:
  1.3 1.6 %pick.1 = bf16[64,16,128]{2,1,0:T(8,128)(2,1)} custom-call(s32[1]{0:T(128)S(6)} %copy.15.live.refs_0_, s32[1,64]{1,0:T(1,128)} %send_block.3, s32[1,64]{1,0:T(1,128)} %send_live.3, bf16[16,2048]{1,0:T(8,128)(2,1)} %feats.3), custom_call_target="tpu_custom_call" | custom-call | bytes 327680 | tf_op jit(solution)/shard_map/pick/pallas_call | solution.py:282
  2.9 14.8 %all-to-all-start = ((bf16[64,2,8,128]{3,2,1,0:T(8,128)(2,1)}), bf16[64,2,8,128]{3,2,1,0:T(8,128)(2,1)S(1)}, u32[]{:S(2)}, u32[]{:S(2)}) async-start(bf16[64,2,8,128]{3,2,1,0:T(8,128)(2,1)} %bitcast.19), calls=%async_computation | async-start | bytes 524288 | tf_op jit(solution)/shard_map/all_to_all | solution.py:280
  17.8 4.5 %local_fwd.1 = (f32[16,16,128]{2,1,0:T(8,128)S(1)}, bf16[16,16,128]{2,1,0:T(8,128)(2,1)S(1)}, bf16[256,256]{1,0:T(8,128)(2,1)S(1)}, bf16[256,256]{1,0:T(8,128)(2...) custom-call(s32[1]{0:T(128)S(6)} %copy.15.live.refs_0_, ...), custom_call_target="tpu_custom_call" | custom-call | flops 12582912 | bytes 4194304 | tf_op jit(solution)/shard_map/local_fwd/pallas_call | solution.py:295
  22.2 7.5 %all-to-all-done = bf16[64,2,8,128]{3,2,1,0:T(8,128)(2,1)S(1)} async-done(((bf16[64,2,8,128]{3,2,1,0:T(8,128)(2,1)}), bf16[64,2,8,128]{3,2,1,0:T(8,128)(2,1)S(1)}, u32[]{:S(2)}, u32[]{:S(2)}) %all-to-all-start) | async-done | bytes 262176 | tf_op jit(solution)/shard_map/all_to_all | solution.py:280
  29.8 0.0 copy-start
  29.8 0.0 copy-start.1
  29.8 0.7 agg.1
  30.5 14.5 %all_to_all.25.got = bf16[8,32,256]{2,1,0:T(8,128)(2,1)S(1)} all-to-all(bf16[8,32,256]{2,1,0:T(8,128)(2,1)S(1)} %agg.1), channel_id=1, replica_groups=mesh['dom'=64,'col'=8] {'col'}, dimensions={0} | all-to-all | bytes 262144 | tf_op jit(solution)/shard_map/all_to_all | solution.py:280
  45.0 0.5 dense.1
  45.5 11.9 %all_to_all.26 = bf16[8,17,8,128]{3,2,1,0:T(8,128)(2,1)S(1)} all-to-all(bf16[8,17,8,128]{3,2,1,0:T(8,128)(2,1)S(1)} %bitcast.18), channel_id=1, replica_groups=mesh['dom'=64,'col'=8] {'col'}, dimensions={0} | all-to-all | bytes 557056 | tf_op jit(solution)/shard_map/all_to_all | solution.py:280
  57.5 0.0 copy-done
  57.5 0.0 copy-done.1
  57.5 0.9 %back.1 = (bf16[8,200,128]{2,1,0:T(8,128)(2,1)S(1)}, f32[16,16,128]{2,1,0:T(8,128)S(1)}, bf16[256,256]{1,0:T(8,128)(2,1)}) custom-call(s32[5,64]{1,0:T(8,128)S(4)} %get-tuple-element.22.places.refs_1_, bf16[8,136,128]{2,1,0:T(8,128)(2,1)S(1)} %bitcast.15, bf16[64,128,128]{2,1,0:T(8,128)(2,1)S(1)} %copy-done, bf16[24,128,128]{2,1,0:T(8,128)(2,1)S(1)} %copy-done.1, ...), custom_call_target="tpu_custom_call" | custom-call | flops 46137344 | bytes 4194304 | tf_op jit(solution)/shard_map/back/pallas_call | solution.py:352
  58.4 14.5 %all_to_all.27 = bf16[8,25,8,128]{3,2,1,0:T(8,128)(2,1)S(1)} all-to-all(bf16[8,25,8,128]{3,2,1,0:T(8,128)(2,1)S(1)} %bitcast.17), channel_id=1, replica_groups={{0,16,32,48,64,80,96,112},{8,24,40,56,72,88,104,120},{128,144,160,176,1..., dimensions={0} | all-to-all | bytes 819200 | tf_op jit(solution)/shard_map/all_to_all | solution.py:280
  72.9 16.0 %all_to_all.28 = bf16[8,25,8,128]{3,2,1,0:T(8,128)(2,1)S(1)} all-to-all(bf16[8,25,8,128]{3,2,1,0:T(8,128)(2,1)S(1)} %bitcast.14), channel_id=1, replica_groups={{0,8,128,136,256,264,384,392},{16,24,144,152,272,280,400,408},{32,40,16..., dimensions={0} | all-to-all | bytes 819200 | tf_op jit(solution)/shard_map/all_to_all | solution.py:280
  88.9 0.8 final.1
  (1 shorter events, 0.0 us)
Async XLA Ops:
  2.9 26.9 %all-to-all-start = ((bf16[64,2,8,128]{3,2,1,0:T(8,128)(2,1)}), bf16[64,2,8,128]{3,2,1,0:T(8,128)(2,1)S(1)}, u32[]{:S(2)}, u32[]{:S(2)}) async-start(bf16[64,2,8,128]{3,2,1,0:T(8,128)(2,1)} %bitcast.19), calls=%async_computation | async-start | bytes 524288 | tf_op jit(solution)/shard_map/all_to_all | solution.py:280
  29.8 27.7 %copy-start = (bf16[64,128,128]{2,1,0:T(8,128)(2,1)S(1)}, bf16[64,128,128]{2,1,0:T(8,128)(2,1)}, u32[]{:S(2)}) copy-start(bf16[64,128,128]{2,1,0:T(8,128)(2,1)} %get-tuple-element.31.rem) | copy-start | bytes 6291460
  29.8 27.7 %copy-start.1 = (bf16[24,128,128]{2,1,0:T(8,128)(2,1)S(1)}, bf16[24,128,128]{2,1,0:T(8,128)(2,1)}, u32[]{:S(2)}) copy-start(bf16[24,128,128]{2,1,0:T(8,128)(2,1)} %get-tuple-element.32.vals) | copy-start | bytes 2359300

commit v8 on v5

--- a/solution.py
+++ b/solution.py
@@ -15,7 +15,7 @@
 ROWS = 16
 H = 256
 LOC = 24
-WAYS = 4
+WAYS = 2
 PART = 16
 G = NX * NCORE
 DW = NZ * ROWS

time: 90.4 us -> 90.4 us (level)
  no operation moved by 1% of the time
where the time goes in v8:
time: 90.4 us; the launch traced here: 90 us
  blocking collectives  57.2 us (63%)
  starting transfers between devices  14.8 us (16%)
  Pallas kernels  9.09 us (10%)
  waiting for transfers between devices  7.54 us (8%)
  between operations  1.34 us (1%)
    all_to_all x4, blocking collectives, swap(): lax.all_to_all(x, axis, split_axis=0, concat_axis=0, tiled=True, axis_ind...  57.2 us
    all_to_all x1, starting transfers between devices, swap(): lax.all_to_all(x, axis, split_axis=0, concat_axis=0, tiled=True, axis_ind...  14.8 us
    all_to_all x1, waiting for transfers between devices, swap(): lax.all_to_all(x, axis, split_axis=0, concat_axis=0, tiled=True, axis_ind...  7.54 us
    pallas_call x1, Pallas kernels, shards(): call(local_fwd_kernel, [pltpu.VMEM((NB, ROWS, W), F32), pltpu.VMEM((NB, R...  4.45 us
  transfers between devices with their start and end apart: 1, of which 1 were waited for; matrix products, arithmetic and copies ran while one was open for 0% of the time, Pallas kernels for 5%

profile of v8, /device:TPU:1, one launch (start us, length us, event | category | flops | bytes accessed | tf_op | source)
XLA Modules:
  0.0 90.0 jit_solution(7455720064055582622)
XLA Ops:
  1.3 1.6 %pick.1 = bf16[64,16,128]{2,1,0:T(8,128)(2,1)} custom-call(s32[1]{0:T(128)S(6)} %copy.15.live.refs_0_, s32[1,64]{1,0:T(1,128)} %send_block.3, s32[1,64]{1,0:T(1,128)} %send_live.3, bf16[16,2048]{1,0:T(8,128)(2,1)} %feats.3), custom_call_target="tpu_custom_call" | custom-call | bytes 327680 | tf_op jit(solution)/shard_map/pick/pallas_call | solution.py:282
  2.9 14.8 %all-to-all-start = ((bf16[64,16,128]{2,1,0:T(8,128)(2,1)}), bf16[64,16,128]{2,1,0:T(8,128)(2,1)S(1)}, u32[]{:S(2)}, u32[]{:S(2)}) async-start(bf16[64,16,128]{2,1,0:T(8,128)(2,1)} %pick.1), calls=%async_computation | async-start | bytes 524288 | tf_op jit(solution)/shard_map/all_to_all | solution.py:280
  17.8 4.5 %local_fwd.1 = (f32[16,16,128]{2,1,0:T(8,128)S(1)}, bf16[16,16,128]{2,1,0:T(8,128)(2,1)S(1)}, bf16[256,256]{1,0:T(8,128)(2,1)S(1)}, bf16[256,256]{1,0:T(8,128)(2...) custom-call(s32[1]{0:T(128)S(6)} %copy.15.live.refs_0_, ...), custom_call_target="tpu_custom_call" | custom-call | flops 12582912 | bytes 4194304 | tf_op jit(solution)/shard_map/local_fwd/pallas_call | solution.py:295
  22.2 7.5 %all-to-all-done.arrived = bf16[64,16,128]{2,1,0:T(8,128)(2,1)S(1)} async-done(((bf16[64,16,128]{2,1,0:T(8,128)(2,1)}), bf16[64,16,128]{2,1,0:T(8,128)(2,1)S(1)}, u32[]{:S(2)}, u32[]{:S(2)}) %all-to-all-start) | async-done | bytes 262176 | tf_op jit(solution)/shard_map/all_to_all | solution.py:280
  29.8 0.0 copy-start
  29.8 0.0 copy-start.1
  29.8 0.7 agg.1
  30.5 14.5 %all_to_all.25.got = bf16[8,32,256]{2,1,0:T(8,128)(2,1)S(1)} all-to-all(bf16[8,32,256]{2,1,0:T(8,128)(2,1)S(1)} %agg.1), channel_id=1, replica_groups=mesh['dom'=64,'col'=8] {'col'}, dimensions={0} | all-to-all | bytes 262144 | tf_op jit(solution)/shard_map/all_to_all | solution.py:280
  45.0 0.5 dense.1
  45.5 12.1 %all_to_all.26.got = bf16[8,144,128]{2,1,0:T(8,128)(2,1)S(1)} all-to-all(bf16[8,144,128]{2,1,0:T(8,128)(2,1)S(1)} %get-tuple-element.30), channel_id=1, replica_groups=mesh['dom'=64,'col'=8] {'col'}, dimensions={0} | all-to-all | bytes 589824 | tf_op jit(solution)/shard_map/all_to_all | solution.py:280
  57.6 0.0 copy-done
  57.6 0.0 copy-done.1
  57.6 0.9 %back.1 = (bf16[8,200,128]{2,1,0:T(8,128)(2,1)S(1)}, f32[16,16,128]{2,1,0:T(8,128)S(1)}, bf16[256,256]{1,0:T(8,128)(2,1)}) custom-call(s32[5,64]{1,0:T(8,128)S(4)} %get-tuple-element.22.places.refs_1_, bf16[8,144,128]{2,1,0:T(8,128)(2,1)S(1)} %all_to_all.26.got, bf16[64,128,128]{2,1,0:T(8,128)(2,1)S(1)} %copy-done, bf16[24,128,128]{2,1,0:T(8,128)(2,1)S(1)} %copy-done.1, ...), custom_call_target="tpu_custom_call" | custom-call | flops 46137344 | bytes 4194304 | tf_op jit(solution)/shard_map/back/pallas_call | solution.py:352
  58.5 14.5 %all_to_all.27.got = bf16[8,200,128]{2,1,0:T(8,128)(2,1)S(1)} all-to-all(bf16[8,200,128]{2,1,0:T(8,128)(2,1)S(1)} %get-tuple-element.36), channel_id=1, replica_groups={{0,16,32,48,64,80,96,112},{8,24,40,56,72,88,104,120},{128,144,160,176,1..., dimensions={0} | all-to-all | bytes 819200 | tf_op jit(solution)/shard_map/all_to_all | solution.py:280
  73.0 16.1 %all_to_all.28.refs_3_ = bf16[8,200,128]{2,1,0:T(8,128)(2,1)S(1)} all-to-all(bf16[8,200,128]{2,1,0:T(8,128)(2,1)S(1)} %turn.1), channel_id=1, replica_groups={{0,8,128,136,256,264,384,392},{16,24,144,152,272,280,400,408},{32,40,16..., dimensions={0} | all-to-all | bytes 819200 | tf_op jit(solution)/shard_map/all_to_all | solution.py:280
  89.1 0.9 final.1
  (1 shorter events, 0.0 us)
Async XLA Ops:
  2.9 26.9 %all-to-all-start = ((bf16[64,16,128]{2,1,0:T(8,128)(2,1)}), bf16[64,16,128]{2,1,0:T(8,128)(2,1)S(1)}, u32[]{:S(2)}, u32[]{:S(2)}) async-start(bf16[64,16,128]{2,1,0:T(8,128)(2,1)} %pick.1), calls=%async_computation | async-start | bytes 524288 | tf_op jit(solution)/shard_map/all_to_all | solution.py:280
  29.8 27.8 %copy-start = (bf16[64,128,128]{2,1,0:T(8,128)(2,1)S(1)}, bf16[64,128,128]{2,1,0:T(8,128)(2,1)}, u32[]{:S(2)}) copy-start(bf16[64,128,128]{2,1,0:T(8,128)(2,1)} %get-tuple-element.31.rem) | copy-start | bytes 6291460
  29.8 27.8 %copy-start.1 = (bf16[24,128,128]{2,1,0:T(8,128)(2,1)S(1)}, bf16[24,128,128]{2,1,0:T(8,128)(2,1)}, u32[]{:S(2)}) copy-start(bf16[24,128,128]{2,1,0:T(8,128)(2,1)} %get-tuple-element.32.vals) | copy-start | bytes 2359300

commit v9 on v5

--- a/solution.py
+++ b/solution.py
@@ -16,7 +16,7 @@
 H = 256
 LOC = 24
 WAYS = 4
-PART = 16
+PART = 32
 G = NX * NCORE
 DW = NZ * ROWS
 DB = DW + 4 * ROWS

time: 90.4 us -> 90.4 us (level)
  no operation moved by 1% of the time
where the time goes in v9:
time: 90.4 us; the launch traced here: 90 us
  blocking collectives  57.2 us (63%)
  starting transfers between devices  14.8 us (16%)
  Pallas kernels  9.14 us (10%)
  waiting for transfers between devices  7.49 us (8%)
  between operations  1.34 us (1%)
    all_to_all x4, blocking collectives, swap(): lax.all_to_all(x, axis, split_axis=0, concat_axis=0, tiled=True, axis_ind...  57.2 us
    all_to_all x1, starting transfers between devices, swap(): lax.all_to_all(x, axis, split_axis=0, concat_axis=0, tiled=True, axis_ind...  14.8 us
    all_to_all x1, waiting for transfers between devices, swap(): lax.all_to_all(x, axis, split_axis=0, concat_axis=0, tiled=True, axis_ind...  7.49 us
    pallas_call x1, Pallas kernels, shards(): call(local_fwd_kernel, [pltpu.VMEM((NB, ROWS, W), F32), pltpu.VMEM((NB, R...  4.5 us
  transfers between devices with their start and end apart: 1, of which 1 were waited for; matrix products, arithmetic and copies ran while one was open for 0% of the time, Pallas kernels for 5%

profile of v9, /device:TPU:1, one launch (start us, length us, event | category | flops | bytes accessed | tf_op | source)
XLA Modules:
  0.0 90.0 jit_solution(13060444937110470370)
XLA Ops:
  1.3 1.6 %pick.1 = bf16[64,16,128]{2,1,0:T(8,128)(2,1)} custom-call(s32[1]{0:T(128)S(6)} %copy.15.live.refs_0_, s32[1,64]{1,0:T(1,128)} %send_block.3, s32[1,64]{1,0:T(1,128)} %send_live.3, bf16[16,2048]{1,0:T(8,128)(2,1)} %feats.3), custom_call_target="tpu_custom_call" | custom-call | bytes 327680 | tf_op jit(solution)/shard_map/pick/pallas_call | solution.py:282
  2.9 14.8 %all-to-all-start = ((bf16[64,16,128]{2,1,0:T(8,128)(2,1)}), bf16[64,16,128]{2,1,0:T(8,128)(2,1)S(1)}, u32[]{:S(2)}, u32[]{:S(2)}) async-start(bf16[64,16,128]{2,1,0:T(8,128)(2,1)} %pick.1), calls=%async_computation | async-start | bytes 524288 | tf_op jit(solution)/shard_map/all_to_all | solution.py:280
  17.8 4.5 %local_fwd.1 = (f32[16,16,128]{2,1,0:T(8,128)S(1)}, bf16[16,16,128]{2,1,0:T(8,128)(2,1)S(1)}, bf16[256,256]{1,0:T(8,128)(2,1)S(1)}, bf16[256,256]{1,0:T(8,128)(2...) custom-call(s32[1]{0:T(128)S(6)} %copy.15.live.refs_0_, ...), custom_call_target="tpu_custom_call" | custom-call | flops 12582912 | bytes 4194304 | tf_op jit(solution)/shard_map/local_fwd/pallas_call | solution.py:295
  22.3 7.5 %all-to-all-done.arrived = bf16[64,16,128]{2,1,0:T(8,128)(2,1)S(1)} async-done(((bf16[64,16,128]{2,1,0:T(8,128)(2,1)}), bf16[64,16,128]{2,1,0:T(8,128)(2,1)S(1)}, u32[]{:S(2)}, u32[]{:S(2)}) %all-to-all-start) | async-done | bytes 262176 | tf_op jit(solution)/shard_map/all_to_all | solution.py:280
  29.8 0.0 copy-start
  29.8 0.0 copy-start.1
  29.8 0.7 agg.1
  30.5 14.5 %all_to_all.25.got = bf16[8,32,256]{2,1,0:T(8,128)(2,1)S(1)} all-to-all(bf16[8,32,256]{2,1,0:T(8,128)(2,1)S(1)} %agg.1), channel_id=1, replica_groups=mesh['dom'=64,'col'=8] {'col'}, dimensions={0} | all-to-all | bytes 262144 | tf_op jit(solution)/shard_map/all_to_all | solution.py:280
  45.0 0.5 dense.1
  45.5 12.0 %all_to_all.26.got = bf16[8,144,128]{2,1,0:T(8,128)(2,1)S(1)} all-to-all(bf16[8,144,128]{2,1,0:T(8,128)(2,1)S(1)} %get-tuple-element.30), channel_id=1, replica_groups=mesh['dom'=64,'col'=8] {'col'}, dimensions={0} | all-to-all | bytes 589824 | tf_op jit(solution)/shard_map/all_to_all | solution.py:280
  57.6 0.0 copy-done
  57.6 0.0 copy-done.1
  57.6 0.9 %back.1 = (bf16[8,200,128]{2,1,0:T(8,128)(2,1)S(1)}, f32[16,16,128]{2,1,0:T(8,128)S(1)}, bf16[256,256]{1,0:T(8,128)(2,1)}) custom-call(s32[5,64]{1,0:T(8,128)S(4)} %get-tuple-element.22.places.refs_1_, bf16[8,144,128]{2,1,0:T(8,128)(2,1)S(1)} %all_to_all.26.got, bf16[64,128,128]{2,1,0:T(8,128)(2,1)S(1)} %copy-done, bf16[24,128,128]{2,1,0:T(8,128)(2,1)S(1)} %copy-done.1, ...), custom_call_target="tpu_custom_call" | custom-call | flops 46137344 | bytes 4194304 | tf_op jit(solution)/shard_map/back/pallas_call | solution.py:352
  58.5 14.4 %all_to_all.27.got = bf16[8,200,128]{2,1,0:T(8,128)(2,1)S(1)} all-to-all(bf16[8,200,128]{2,1,0:T(8,128)(2,1)S(1)} %get-tuple-element.36), channel_id=1, replica_groups={{0,16,32,48,64,80,96,112},{8,24,40,56,72,88,104,120},{128,144,160,176,1..., dimensions={0} | all-to-all | bytes 819200 | tf_op jit(solution)/shard_map/all_to_all | solution.py:280
  73.0 16.1 %all_to_all.28.refs_3_ = bf16[8,200,128]{2,1,0:T(8,128)(2,1)S(1)} all-to-all(bf16[8,200,128]{2,1,0:T(8,128)(2,1)S(1)} %turn.1), channel_id=1, replica_groups={{0,8,128,136,256,264,384,392},{16,24,144,152,272,280,400,408},{32,40,16..., dimensions={0} | all-to-all | bytes 819200 | tf_op jit(solution)/shard_map/all_to_all | solution.py:280
  89.1 0.8 final.1
  (1 shorter events, 0.0 us)
Async XLA Ops:
  2.9 26.9 %all-to-all-start = ((bf16[64,16,128]{2,1,0:T(8,128)(2,1)}), bf16[64,16,128]{2,1,0:T(8,128)(2,1)S(1)}, u32[]{:S(2)}, u32[]{:S(2)}) async-start(bf16[64,16,128]{2,1,0:T(8,128)(2,1)} %pick.1), calls=%async_computation | async-start | bytes 524288 | tf_op jit(solution)/shard_map/all_to_all | solution.py:280
  29.8 27.8 %copy-start = (bf16[64,128,128]{2,1,0:T(8,128)(2,1)S(1)}, bf16[64,128,128]{2,1,0:T(8,128)(2,1)}, u32[]{:S(2)}) copy-start(bf16[64,128,128]{2,1,0:T(8,128)(2,1)} %get-tuple-element.31.rem) | copy-start | bytes 6291460
  29.8 27.8 %copy-start.1 = (bf16[24,128,128]{2,1,0:T(8,128)(2,1)S(1)}, bf16[24,128,128]{2,1,0:T(8,128)(2,1)}, u32[]{:S(2)}) copy-start(bf16[24,128,128]{2,1,0:T(8,128)(2,1)} %get-tuple-element.32.vals) | copy-start | bytes 2359300
